TPU v7x, 32 devices: a whole 2x2x4 slice. The times are simulated.
32 devices in a mesh: tm: 8 (over y, x, core), band: 4 (over z).
Axes of the slice: x: 2, y: 2, z: 4, core: 2. Of those that a mesh axis runs over, the one named last changes fastest.
Arguments:
- video: bfloat16 [8, 16, 104, 384], P('tm', 'band'), may hold values from -6 to 6
- past_first: bfloat16 [2, 16, 104, 384], P(None, 'band'), may hold values from -6 to 6
- past_second: bfloat16 [2, 16, 104, 384], P(None, 'band'), may hold values from -6 to 6
- conv_first: bfloat16 [3, 3, 3, 384, 384], P(None, None, None, 'tm'), may hold values from -0.0625 to 0.0625
- bias_first: float32 [384], replicated, may hold values from -3 to 3
- conv_second: bfloat16 [3, 3, 3, 384, 384], P(None, None, None, 'tm'), may hold values from -0.0625 to 0.0625
- bias_second: float32 [384], replicated, may hold values from -3 to 3
- gain_first: float32 [384], replicated, may hold values from 0.1 to 1.9
- gain_second: float32 [384], replicated, may hold values from 0.1 to 1.9
- gain_attn: float32 [384], replicated, may hold values from 0.1 to 1.9
- query_weight: bfloat16 [384, 384], replicated, may hold values from -1.5 to 4.5
- key_weight: bfloat16 [384, 384], replicated, may hold values from -1.5 to 4.5
- value_weight: bfloat16 [384, 384], replicated, may hold values from -0.3125 to 0.3125
- out_weight: bfloat16 [384, 384], replicated, may hold values from -0.3125 to 0.3125
Outputs:
- encoded: bfloat16 [8, 16, 104, 384], P('tm', 'band')
All inputs are finite; a program needn't handle non-finite values.
Results may differ from a plain program's by a relative error of at most 0.012.
Values may be sent and summed in bfloat16 or wider, within the bound.
A program may use at most 128 MiB of HBM per device.

v0:
```python
import jax
import jax.numpy as jnp
from jax import lax
from jax.sharding import PartitionSpec as P


def extended_2(block, sides, width):
    for axis, dim in sides:
        count = lax.axis_size(axis)
        forward = [(i, i + 1) for i in range(count - 1)]
        backward = [(target, source) for source, target in forward]
        low = lax.ppermute(
            lax.slice_in_dim(block, block.shape[dim] - width, None, axis=dim), axis, forward
        )
        high = lax.ppermute(lax.slice_in_dim(block, 0, width, axis=dim), axis, backward)
        block = jnp.concatenate([low, block, high], axis=dim)
    return block


def from_behind(x, axis, by):
    devices = lax.axis_size(axis)
    pairs = [(i, i + by) for i in range(devices) if 0 <= i + by < devices]
    return lax.ppermute(x, axis, pairs)


def normalize(values_f32, gain):
    return (
        values_f32
        * lax.rsqrt(jnp.mean(values_f32 * values_f32, axis=-1, keepdims=True) + 1e-06)
        * gain
    )


def edge_rows(stacked):
    return extended_2(stacked, (("band", 1),), 1)


def unfold(frames, rows_out):
    width = frames.shape[2] - 2
    windows = []
    for tap_t in range(3):
        for tap_r in range(3):
            for tap_c in range(3):
                windows.append(frames[tap_t, tap_r : tap_r + rows_out, tap_c : tap_c + width, :])
    columns = jnp.concatenate(windows, axis=-1)
    return columns.reshape(rows_out * width, columns.shape[-1])


def time_frames(extended):
    current = extended[2:3]
    one_prior = from_behind(current, "tm", 1)
    two_prior = from_behind(current, "tm", 2)
    position = lax.axis_index("tm")
    back_one = jnp.where(position == 0, extended[1:2], one_prior)
    back_two = jnp.where(
        position == 0, extended[0:1], jnp.where(position == 1, extended[1:2], two_prior)
    )
    return jnp.concatenate([back_two, back_one, current], axis=0)


def convolve(extended, kernel, bias):
    rows_out = extended.shape[1] - 2
    width = extended.shape[2]
    out_chans = kernel.shape[4]
    frames = jnp.pad(time_frames(extended), ((0, 0), (0, 0), (1, 1), (0, 0)))
    kernel_piece = lax.all_gather(kernel, "tm", axis=3, tiled=True)
    share = kernel_piece.shape[3]
    columns = unfold(frames, rows_out)
    flat = kernel_piece.reshape(27 * share, out_chans)
    summed = jnp.dot(columns, flat, preferred_element_type=jnp.float32)
    result = summed.reshape(1, rows_out, width, out_chans)
    return result + bias


def local(
    video,
    past_first,
    past_second,
    conv_first,
    bias_first,
    conv_second,
    bias_second,
    gain_first,
    gain_second,
    gain_attn,
    query_weight,
    key_weight,
    value_weight,
    out_weight,
):
    row_count = video.shape[1]
    col_count = video.shape[2]
    chan_count = video.shape[3]
    video_f32 = video.astype(jnp.float32)
    first_act = jax.nn.silu(normalize(video_f32, gain_first)).astype(jnp.bfloat16)
    stack_one = jnp.concatenate([past_first, first_act], axis=0)
    hidden = convolve(edge_rows(stack_one), conv_first, bias_first)
    second_act = jax.nn.silu(normalize(hidden, gain_second)).astype(jnp.bfloat16)
    ext_two = edge_rows(jnp.concatenate([past_second, second_act], axis=0))
    conv_out = convolve(ext_two, conv_second, bias_second)
    block_out = (video_f32 + conv_out).astype(jnp.bfloat16)
    token_rows = block_out.reshape(row_count * col_count, chan_count)
    normed = normalize(token_rows.astype(jnp.float32), gain_attn).astype(jnp.bfloat16)
    queries = jnp.dot(normed, query_weight, preferred_element_type=jnp.float32).astype(jnp.bfloat16)
    factor = 1.0 / jnp.sqrt(jnp.float32(chan_count))
    token_count = queries.shape[0]
    key_rows = jnp.dot(normed, key_weight, preferred_element_type=jnp.float32).astype(jnp.bfloat16)
    value_rows = jnp.dot(normed, value_weight, preferred_element_type=jnp.float32).astype(
        jnp.bfloat16
    )
    top_prev = jnp.full((token_count,), -jnp.inf, jnp.float32)
    total_prev = jnp.zeros((token_count,), jnp.float32)
    accum = jnp.zeros((token_count, chan_count), jnp.float32)
    scores = (
        jnp.dot(
            queries,
            lax.all_gather(key_rows, "band", axis=0, tiled=True).T,
            preferred_element_type=jnp.float32,
        )
        * factor
    )
    top_next = jnp.max(scores, axis=1)
    shrink = jnp.exp(top_prev - top_next)
    expo = jnp.exp(scores - top_next[:, None])
    total_next = total_prev * shrink + jnp.sum(expo, axis=1)
    accum = accum * shrink[:, None] + jnp.dot(
        expo.astype(jnp.bfloat16),
        lax.all_gather(value_rows, "band", axis=0, tiled=True),
        preferred_element_type=jnp.float32,
    )
    att = (accum / total_next[:, None]).astype(jnp.bfloat16)
    projected = jnp.dot(att, out_weight, preferred_element_type=jnp.float32)
    encoded = (token_rows.astype(jnp.float32) + projected).astype(jnp.bfloat16)
    return encoded.reshape(1, row_count, col_count, chan_count)


def solution(mesh):
    return jax.shard_map(
        local,
        mesh=mesh,
        in_specs=(
            P("tm", "band", None, None),
            P(None, "band", None, None),
            P(None, "band", None, None),
            P(None, None, None, "tm", None),
            P(),
            P(None, None, None, "tm", None),
            P(),
            P(),
            P(),
            P(),
            P(),
            P(),
            P(),
            P(),
        ),
        out_specs=P("tm", "band", None, None),
        check_vma=False,
    )
```

profile of v0, /device:TPU:0, one launch (start us, length us, event | category | flops | bytes accessed | tf_op | source)
XLA Modules:
  0.0 248.1 jit_solution(15894968146222201222)
XLA Ops:
  7.3 1.1 fusion.27
  8.4 1.2 fusion.34
  9.7 1.1 pad_maximum_fusion.13
  10.8 4.9 %collective-permute-start = (bf16[3,1,104,384]{3,2,1,0:T(8,128)(2,1)S(1)}, bf16[3,1,104,384]{3,2,1,0:T(8,128)(2,1)S(1)}, u32[]{:S(2)}, u32[]{:S(2)}) collective-permute-start(bf16[3,1,104,384]{3,2,1,0:T(8,128)(2,1)S(1)} %get-tuple-element.11), channel_id=1, source_target_pairs={{0,1},{1,2},{2,3},{4,5},{5,6},{6,7},{8,9},{9,10},{10,11},{12,13},{... | collective-permute-start | bytes 718856 | tf_op jit(solution)/shard_map/ppermute | solution.py:12
  15.7 1.3 collective-permute-start.1
  17.0 3.7 %collective-permute-done = bf16[3,1,104,384]{3,2,1,0:T(8,128)(2,1)S(1)} collective-permute-done((bf16[3,1,104,384]{3,2,1,0:T(8,128)(2,1)S(1)}, bf16[3,1,104,384]{3,2,1,0:T(8,128)(2,1)S(1)}, u32[]{:S(2)}, u32[]{:S(2)}) %collective-permute-start) | collective-permute-done | bytes 239648 | tf_op jit(solution)/shard_map/ppermute | solution.py:12
  20.8 4.1 %collective-permute-done.1 = bf16[3,1,104,384]{3,2,1,0:T(8,128)(2,1)S(1)} collective-permute-done((bf16[3,1,104,384]{3,2,1,0:T(8,128)(2,1)S(1)}, bf16[3,1,104,384]{3,2,1,0:T(8,128)(2,1)S(1)}, u32[]{:S(2)}, u32[]{:S(2)}) %collective-permute-start.1) | collective-permute-done | bytes 239648 | tf_op jit(solution)/shard_map/ppermute | solution.py:15
  24.9 1.3 pad_maximum_fusion
  26.3 4.2 %collective-permute-start.2 = (bf16[1,6,104,384]{3,2,1,0:T(8,128)(2,1)S(1)}, bf16[1,6,104,384]{3,2,1,0:T(8,128)(2,1)}, u32[]{:S(2)}, u32[]{:S(2)}) collective-permute-start(bf16[1,6,104,384]{3,2,1,0:T(8,128)(2,1)S(1)} %slice.302), channel_id=1, source_target_pairs={{0,8},{4,12},{8,16},{12,20},{16,24},{20,28},{1,9},{5,13},{9,17},{1... | collective-permute-start | bytes 1437704 | tf_op jit(solution)/shard_map/ppermute | solution.py:23
  30.5 2.1 collective-permute-start.3
  32.6 9.3 %collective-permute-done.2 = bf16[1,6,104,384]{3,2,1,0:T(8,128)(2,1)} collective-permute-done((bf16[1,6,104,384]{3,2,1,0:T(8,128)(2,1)S(1)}, bf16[1,6,104,384]{3,2,1,0:T(8,128)(2,1)}, u32[]{:S(2)}, u32[]{:S(2)}) %collective-permute-start.2) | collective-permute-done | bytes 479264 | tf_op jit(solution)/shard_map/ppermute | solution.py:23
  41.9 1.3 slice_select_fusion.1
  61.6 1.0 bitcast_dynamic-update-slice_fusion
  62.6 0.9 fusion.69
  65.9 5.5 %all-gather.5.cloned.1.call-done = bf16[3,3,3,384,384]{4,3,2,1,0:T(8,128)(2,1)} async-done(((bf16[3,3,3,48,384]{4,3,2,1,0:T(8,128)(2,1)}), bf16[3,3,3,384,384]{4,3,2,1,0:T(8,128)(2,1)}) %all-gather.5.cloned.1.call-update) | async-done | bytes 7962640 | tf_op jit(solution)/shard_map/all_gather | solution.py:66
  71.4 9.9 %multiply_reduce_fusion.1 = (f32[4,104]{1,0:T(4,128)S(1)}, f32[4,104,384]{2,1,0:T(8,128)S(1)}) fusion(f32[384]{0:T(512)S(1)} %copy-done.10, bf16[4,104,10368]{2,1,0:T(8,128)(2,1)} %fusion.65, bf16[10368,384,1]{1,0,2:T(8,128)(2,1)} %bitcast.248), kind=kOutput, calls=%fused_computation.47 | convolution fusion | flops 3312930304 | bytes 17230976 | tf_op jit(solution)/shard_map/dot_general | solution.py:70
  81.7 3.4 %collective-permute-start.4 = (bf16[3,1,104,384]{3,2,1,0:T(8,128)(2,1)S(1)}, bf16[3,1,104,384]{3,2,1,0:T(8,128)(2,1)S(1)}, u32[]{:S(2)}, u32[]{:S(2)}) collective-permute-start(bf16[3,1,104,384]{3,2,1,0:T(8,128)(2,1)S(1)} %get-tuple-element.9), channel_id=1, source_target_pairs={{0,1},{1,2},{2,3},{4,5},{5,6},{6,7},{8,9},{9,10},{10,11},{12,13},{... | collective-permute-start | bytes 718856 | tf_op jit(solution)/shard_map/ppermute | solution.py:12
  85.1 1.3 collective-permute-start.5
  86.4 2.3 collective-permute-done.4
  88.7 4.4 %collective-permute-done.5 = bf16[3,1,104,384]{3,2,1,0:T(8,128)(2,1)S(1)} collective-permute-done((bf16[3,1,104,384]{3,2,1,0:T(8,128)(2,1)S(1)}, bf16[3,1,104,384]{3,2,1,0:T(8,128)(2,1)S(1)}, u32[]{:S(2)}, u32[]{:S(2)}) %collective-permute-start.5) | collective-permute-done | bytes 239648 | tf_op jit(solution)/shard_map/ppermute | solution.py:15
  93.4 12.1 %collective-permute-start.6 = (bf16[1,6,104,384]{3,2,1,0:T(8,128)(2,1)S(1)}, bf16[1,6,104,384]{3,2,1,0:T(8,128)(2,1)S(1)}, u32[]{:S(2)}, u32[]{:S(2)}) collective-permute-start(bf16[1,6,104,384]{3,2,1,0:T(8,128)(2,1)S(1)} %slice.329), channel_id=1, source_target_pairs={{0,8},{4,12},{8,16},{12,20},{16,24},{20,28},{1,9},{5,13},{9,17},{1... | collective-permute-start | bytes 1437704 | tf_op jit(solution)/shard_map/ppermute | solution.py:23
  105.5 1.5 collective-permute-start.7
  107.1 20.0 %collective-permute-done.6 = bf16[1,6,104,384]{3,2,1,0:T(8,128)(2,1)S(1)} collective-permute-done((bf16[1,6,104,384]{3,2,1,0:T(8,128)(2,1)S(1)}, bf16[1,6,104,384]{3,2,1,0:T(8,128)(2,1)S(1)}, u32[]{:S(2)}, u32[]{:S(2)}) %collective-permute-start.6) | collective-permute-done | bytes 479264 | tf_op jit(solution)/shard_map/ppermute | solution.py:23
  141.6 0.9 fusion.47
  145.7 1.0 constant_dynamic-update-slice_fusion
  150.1 9.8 %multiply_reduce_fusion = (f32[4,104]{1,0:T(4,128)S(1)}, f32[1,4,104,384]{3,2,1,0:T(8,128)S(1)}) fusion(f32[384]{0:T(512)S(1)} %copy-done.11, bf16[4,104,10368]{2,1,0:T(8,128)(2,1)} %fusion.37, bf16[10368,384,1]{1,0,2:T(8,128)(2,1)} %bitcast.247, bf16[1,4,104,384]{3,2,1,0:T(8,128)(2,1)S(1)} %copy-done.3), kind=kOutput, calls=%fused_computation.45 | convolution fusion | flops 3313569280 | bytes 17550464 | tf_op jit(solution)/shard_map/dot_general | solution.py:70
  160.1 1.1 convolution_convert_fusion.1
  161.3 1.1 convolution_convert_fusion
  162.4 43.0 %all-gather.9.cloned.1.call-done = bf16[1664,384]{1,0:T(8,128)(2,1)} async-done(((bf16[416,384]{1,0:T(8,128)(2,1)}), bf16[1664,384]{1,0:T(8,128)(2,1)}) %all-gather.9.cloned.1.call-update) | async-done | bytes 1277968 | tf_op jit(solution)/shard_map/all_gather | solution.py:117
  205.4 2.6 %fusion.96 = (f32[416]{0:T(512)S(1)}, f32[416,1664]{1,0:T(8,128)S(1)}) fusion(bf16[1664,384]{1,0:T(8,128)(2,1)} %all-gather.9.cloned.1.call-done, bf16[416,384]{1,0:T(8,128)(2,1)S(1)} %fusion.36, bf16[384,384]{1,0:T(8,128)(2,1)S(1)} %copy-done), kind=kOutput, calls=%fused_computation.177 | convolution fusion | flops 655855232 | bytes 4662912 | tf_op jit(solution)/shard_map/dot_general | solution.py:115
  208.6 29.5 %all-gather.11.cloned.1.call-done = bf16[1664,384]{1,0:T(8,128)(2,1)} async-done(((bf16[416,384]{1,0:T(8,128)(2,1)}), bf16[1664,384]{1,0:T(8,128)(2,1)}) %all-gather.11.cloned.1.call-update) | async-done | bytes 1277968 | tf_op jit(solution)/shard_map/all_gather | solution.py:128
  238.0 3.5 %fusion.16 = bf16[416,384]{1,0:T(8,128)(2,1)} fusion(f32[416,384]{1,0:T(8,128)} %bitcast.246, bf16[384,384]{1,0:T(8,128)(2,1)} %param.27, bf16[1664,384]{1,0:T(8,128)(2,1)} %all-gather.11.cloned.1.call-done, f32[416,1664]{1,0:T(8,128)S(1)} %get-tuple-element.20, f32[416]{0:T(512)S(1)} %get-tuple-element.19, f32[416]{0:T(512)S(1)} %get-tuple-element.14, ...), kind=kOutput, calls=%fused_computation.24 | convolution fusion | flops 656494592 | bytes 5305216 | tf_op jit(solution)/shard_map/dot_general | solution.py:132
  (100 shorter events, 44.2 us)
Async XLA Ops:
  6.5 198.9 %copy-start = (bf16[384,384]{1,0:T(8,128)(2,1)S(1)}, bf16[384,384]{1,0:T(8,128)(2,1)}, u32[]{:S(2)}) copy-start(bf16[384,384]{1,0:T(8,128)(2,1)} %param.24) | copy-start | bytes 884740
  6.5 64.9 %all-gather.5.cloned.1.call-start = ((), (), s32[]{:S(2)}) async-start(), calls=%async_computation | async-start | bytes 8957952 | tf_op jit(solution)/shard_map/all_gather | solution.py:66
  7.3 142.8 %all-gather.7.cloned.1.call-start = ((), (), s32[]{:S(2)}) async-start(), calls=%async_computation.1 | async-start | bytes 8957952 | tf_op jit(solution)/shard_map/all_gather | solution.py:66
  10.8 10.0 %collective-permute-start = (bf16[3,1,104,384]{3,2,1,0:T(8,128)(2,1)S(1)}, bf16[3,1,104,384]{3,2,1,0:T(8,128)(2,1)S(1)}, u32[]{:S(2)}, u32[]{:S(2)}) collective-permute-start(bf16[3,1,104,384]{3,2,1,0:T(8,128)(2,1)S(1)} %get-tuple-element.11), channel_id=1, source_target_pairs={{0,1},{1,2},{2,3},{4,5},{5,6},{6,7},{8,9},{9,10},{10,11},{12,13},{... | collective-permute-start | bytes 718856 | tf_op jit(solution)/shard_map/ppermute | solution.py:12
  15.7 9.2 %collective-permute-start.1 = (bf16[3,1,104,384]{3,2,1,0:T(8,128)(2,1)S(1)}, bf16[3,1,104,384]{3,2,1,0:T(8,128)(2,1)S(1)}, u32[]{:S(2)}, u32[]{:S(2)}) collective-permute-start(bf16[3,1,104,384]{3,2,1,0:T(8,128)(2,1)S(1)} %get-tuple-element.12), channel_id=1, source_target_pairs={{1,0},{2,1},{3,2},{5,4},{6,5},{7,6},{9,8},{10,9},{11,10},{13,12},{... | collective-permute-start | bytes 718856 | tf_op jit(solution)/shard_map/ppermute | solution.py:15
  26.3 15.6 %collective-permute-start.2 = (bf16[1,6,104,384]{3,2,1,0:T(8,128)(2,1)S(1)}, bf16[1,6,104,384]{3,2,1,0:T(8,128)(2,1)}, u32[]{:S(2)}, u32[]{:S(2)}) collective-permute-start(bf16[1,6,104,384]{3,2,1,0:T(8,128)(2,1)S(1)} %slice.302), channel_id=1, source_target_pairs={{0,8},{4,12},{8,16},{12,20},{16,24},{20,28},{1,9},{5,13},{9,17},{1... | collective-permute-start | bytes 1437704 | tf_op jit(solution)/shard_map/ppermute | solution.py:23
  30.5 11.4 %collective-permute-start.3 = (bf16[1,6,104,384]{3,2,1,0:T(8,128)(2,1)S(1)}, bf16[1,6,104,384]{3,2,1,0:T(8,128)(2,1)}, u32[]{:S(2)}, u32[]{:S(2)}) collective-permute-start(bf16[1,6,104,384]{3,2,1,0:T(8,128)(2,1)S(1)} %slice.302), channel_id=1, source_target_pairs={{0,4},{4,8},{8,12},{12,16},{16,20},{20,24},{24,28},{1,5},{5,9},{9,... | collective-permute-start | bytes 1437704 | tf_op jit(solution)/shard_map/ppermute | solution.py:23
  32.6 172.9 %all-gather.9.cloned.1.call-start = ((), (), s32[]{:S(2)}) async-start(), calls=%async_computation.2 | async-start | bytes 1597440 | tf_op jit(solution)/shard_map/all_gather | solution.py:117
  32.6 26.6 %copy-start.1 = (bf16[2,4,104,384]{3,2,1,0:T(8,128)(2,1)S(1)}, bf16[2,4,104,384]{3,2,1,0:T(8,128)(2,1)}, u32[]{:S(2)}) copy-start(bf16[2,4,104,384]{3,2,1,0:T(8,128)(2,1)} %param.15) | copy-start | bytes 1916932
  43.2 18.4 %copy-start.3 = (bf16[1,4,104,384]{3,2,1,0:T(8,128)(2,1)S(1)}, bf16[1,4,104,384]{3,2,1,0:T(8,128)(2,1)}, u32[]{:S(2)}) copy-start(bf16[1,4,104,384]{3,2,1,0:T(8,128)(2,1)} %param.14) | copy-start | bytes 958468
  43.2 18.4 %copy-start.7 = (f32[384]{0:T(512)S(1)}, f32[384]{0:T(512)}, u32[]{:S(2)}) copy-start(f32[384]{0:T(512)} %param.21) | copy-start | bytes 4612
  46.3 25.1 %copy-start.10 = (f32[384]{0:T(512)S(1)}, f32[384]{0:T(512)}, u32[]{:S(2)}) copy-start(f32[384]{0:T(512)} %param.18) | copy-start | bytes 4612
  71.4 9.9 %copy-start.8 = (f32[384]{0:T(512)S(1)}, f32[384]{0:T(512)}, u32[]{:S(2)}) copy-start(f32[384]{0:T(512)} %param.22) | copy-start | bytes 4612
  71.4 10.2 %copy-start.2 = (bf16[2,4,104,384]{3,2,1,0:T(8,128)(2,1)S(1)}, bf16[2,4,104,384]{3,2,1,0:T(8,128)(2,1)}, u32[]{:S(2)}) copy-start(bf16[2,4,104,384]{3,2,1,0:T(8,128)(2,1)} %param.16) | copy-start | bytes 1916932
  81.7 7.0 %collective-permute-start.4 = (bf16[3,1,104,384]{3,2,1,0:T(8,128)(2,1)S(1)}, bf16[3,1,104,384]{3,2,1,0:T(8,128)(2,1)S(1)}, u32[]{:S(2)}, u32[]{:S(2)}) collective-permute-start(bf16[3,1,104,384]{3,2,1,0:T(8,128)(2,1)S(1)} %get-tuple-element.9), channel_id=1, source_target_pairs={{0,1},{1,2},{2,3},{4,5},{5,6},{6,7},{8,9},{9,10},{10,11},{12,13},{... | collective-permute-start | bytes 718856 | tf_op jit(solution)/shard_map/ppermute | solution.py:12
  85.1 8.0 %collective-permute-start.5 = (bf16[3,1,104,384]{3,2,1,0:T(8,128)(2,1)S(1)}, bf16[3,1,104,384]{3,2,1,0:T(8,128)(2,1)S(1)}, u32[]{:S(2)}, u32[]{:S(2)}) collective-permute-start(bf16[3,1,104,384]{3,2,1,0:T(8,128)(2,1)S(1)} %get-tuple-element.10), channel_id=1, source_target_pairs={{1,0},{2,1},{3,2},{5,4},{6,5},{7,6},{9,8},{10,9},{11,10},{13,12},{... | collective-permute-start | bytes 718856 | tf_op jit(solution)/shard_map/ppermute | solution.py:15
  93.4 33.6 %collective-permute-start.6 = (bf16[1,6,104,384]{3,2,1,0:T(8,128)(2,1)S(1)}, bf16[1,6,104,384]{3,2,1,0:T(8,128)(2,1)S(1)}, u32[]{:S(2)}, u32[]{:S(2)}) collective-permute-start(bf16[1,6,104,384]{3,2,1,0:T(8,128)(2,1)S(1)} %slice.329), channel_id=1, source_target_pairs={{0,8},{4,12},{8,16},{12,20},{16,24},{20,28},{1,9},{5,13},{9,17},{1... | collective-permute-start | bytes 1437704 | tf_op jit(solution)/shard_map/ppermute | solution.py:23
  105.5 21.5 %collective-permute-start.7 = (bf16[1,6,104,384]{3,2,1,0:T(8,128)(2,1)S(1)}, bf16[1,6,104,384]{3,2,1,0:T(8,128)(2,1)S(1)}, u32[]{:S(2)}, u32[]{:S(2)}) collective-permute-start(bf16[1,6,104,384]{3,2,1,0:T(8,128)(2,1)S(1)} %slice.329), channel_id=1, source_target_pairs={{0,4},{4,8},{8,12},{12,16},{16,20},{20,24},{24,28},{1,5},{5,9},{9,... | collective-permute-start | bytes 1437704 | tf_op jit(solution)/shard_map/ppermute | solution.py:23
  130.3 19.8 %copy-start.11 = (f32[384]{0:T(512)S(1)}, f32[384]{0:T(512)}, u32[]{:S(2)}) copy-start(f32[384]{0:T(512)} %param.20) | copy-start | bytes 4612
  150.0 9.9 %copy-start.9 = (f32[384]{0:T(512)S(1)}, f32[384]{0:T(512)}, u32[]{:S(2)}) copy-start(f32[384]{0:T(512)} %param.23) | copy-start | bytes 4612
  150.0 10.1 %copy-start.5 = (bf16[384,384]{1,0:T(8,128)(2,1)S(1)}, bf16[384,384]{1,0:T(8,128)(2,1)}, u32[]{:S(2)}) copy-start(bf16[384,384]{1,0:T(8,128)(2,1)} %param.25) | copy-start | bytes 884740
  150.1 11.2 %copy-start.6 = (bf16[384,384]{1,0:T(8,128)(2,1)S(1)}, bf16[384,384]{1,0:T(8,128)(2,1)}, u32[]{:S(2)}) copy-start(bf16[384,384]{1,0:T(8,128)(2,1)} %param.26) | copy-start | bytes 884740
  159.9 2.5 %copy-start.4 = (f32[1,4,104,384]{3,2,1,0:T(8,128)}, f32[1,4,104,384]{3,2,1,0:T(8,128)S(1)}, u32[]{:S(2)}) copy-start(f32[1,4,104,384]{3,2,1,0:T(8,128)S(1)} %get-tuple-element.18) | copy-start | bytes 1916932
  161.2 76.8 %all-gather.11.cloned.1.call-start = ((), (), s32[]{:S(2)}) async-start(), calls=%async_computation.3 | async-start | bytes 1597440 | tf_op jit(solution)/shard_map/all_gather | solution.py:128
Sparse Core Ops, SparseCore 0:
  9.3 62.1 all-gather.4
  73.3 67.4 all-gather.6
  161.4 44.0 all-gather.8
  206.9 31.1 all-gather.10
where the time goes:
time: 249 us; the launch traced here: 248 us
  waiting for transfers between devices  123 us (49%)
  local copies, waits for them, and re-layouts  39.2 us (16%)
  starting transfers between devices  30.9 us (12%)
  matrix products  27.9 us (11%)
  other arithmetic  13.9 us (6%)
  between operations  13.4 us (5%)
    all_gather x1, waiting for transfers between devices, local(): lax.all_gather(key_rows, 'band', axis=0, tiled=True)  43 us
    unnamed x70, local copies, waits for them, and re-layouts  37.4 us
    all_gather x1, waiting for transfers between devices, local(): lax.all_gather(value_rows, 'band', axis=0, tiled=True)  29.5 us
    ppermute x4, waiting for transfers between devices, from_behind(): return lax.ppermute(x, axis, pairs)  29.3 us
    ppermute x4, starting transfers between devices, from_behind(): return lax.ppermute(x, axis, pairs)  19.9 us
    dot_general x2, matrix products, convolve(): summed = jnp.dot(columns, flat, preferred_element_type=jnp.float32)  19.7 us
    ppermute x2, waiting for transfers between devices, extended_2(): lax.ppermute(lax.slice_in_dim(block, 0, width, axis=dim), axis, backward)  8.53 us
    ppermute x2, starting transfers between devices, extended_2(): lax.ppermute(lax.slice_in_dim(block, block.shape[dim] - width, None, axis...  8.35 us
  transfers between devices with their start and end apart: 12, of which 9 were waited for; matrix products, arithmetic and copies ran while one was open for 27% of the time, Pallas kernels for 0%

commit v1 on v0

v1 whole, which is shorter than its diff:
```python
import functools

import jax
import jax.numpy as jnp
from jax import lax
from jax.experimental import pallas as pl
from jax.experimental.pallas import tpu as pltpu
from jax.sharding import PartitionSpec as P

MESH = pl.DeviceIdType.MESH
BF = jnp.bfloat16
F32 = jnp.float32
SLOT = 64
LANES = 2 * SLOT


def normalize(v, gain):
    return v * lax.rsqrt(jnp.mean(v * v, axis=-1, keepdims=True) + 1e-06) * gain


def silu(v):
    return v / (1.0 + jnp.exp(-v))


def kernel(
    chips, bands, rows, cols, wide,
    video, past1, past2, w1, w2, bias1, bias2, gain1, gain2, gain3, select,
    wq, wk, wv, wo, out,
    weights, stage, act, shifted, psend, precv, own, held, queries, top, total, accum,
    wl_sem, ws_sem, wr_sem, ms_sem, mr_sem, hs_sem, hr_sem, qs_sem, qr_sem,
    fs_sem, fr_sem, gs_sem, gr_sem, ps_sem, pr_sem, xr_sem, xright_sem, xleft_sem,
):
    t = lax.axis_index("tm")
    z = lax.axis_index("band")
    chip = t // 2
    core = t % 2
    mate = t + 1 - 2 * core
    last = bands - 1
    cells = rows * cols
    chans = video.shape[1]
    has_low = z > 0
    has_high = z < last

    def remote(src, dst, send, recv, tm, band):
        return pltpu.make_async_remote_copy(
            src_ref=src, dst_ref=dst, send_sem=send, recv_sem=recv,
            device_id=(tm, band), device_id_type=MESH,
        )

    def peer(d):
        return lax.rem(chip + d, chips)

    barrier = pltpu.get_barrier_semaphore()
    pl.semaphore_signal(barrier, inc=1, device_id=(mate, z), device_id_type=MESH)
    for d in range(1, chips):
        pl.semaphore_signal(barrier, inc=1, device_id=(peer(d) * 2 + core, z), device_id_type=MESH)

    @pl.when(has_low)
    def _():
        pl.semaphore_signal(barrier, inc=1, device_id=(t, z - 1), device_id_type=MESH)

    @pl.when(has_high)
    def _():
        pl.semaphore_signal(barrier, inc=1, device_id=(t, z + 1), device_id_type=MESH)

    def local_weight(conv, w):
        return pltpu.make_async_copy(w, weights.at[conv, :, core], wl_sem.at[conv])

    def sent_weight(conv, w):
        return remote(
            w, weights.at[conv, :, core], ws_sem.at[conv], wr_sem.at[conv], mate, z
        )

    def put_stage(conv, values):
        cube = values.reshape(rows, cols, chans)
        cube = jnp.concatenate([cube, jnp.zeros((rows, wide - cols, chans), F32)], axis=1)
        flat = cube.reshape(rows * wide, chans).astype(BF)
        spread = jnp.dot(flat, select[...], preferred_element_type=F32).astype(BF)
        for q in range(chips):
            stage[conv, q] = spread[:, q * LANES : (q + 1) * LANES].reshape(rows, wide, LANES)

    for conv, past in ((0, past1), (1, past2)):
        act[conv, 0, :, 1 : rows + 1] = past[...]

        @pl.when(z == 0)
        def _():
            act[conv, :, :, 0:1] = jnp.zeros((chips + 1, 2, 1, wide, LANES), BF)

        @pl.when(z == last)
        def _():
            act[conv, :, :, rows + 1 : rows + 2] = jnp.zeros((chips + 1, 2, 1, wide, LANES), BF)

    local_weight(0, w1).start()
    local_weight(1, w2).start()
    vid = video[...].astype(F32)
    put_stage(0, silu(normalize(vid, gain1[...])))
    act[0, chip + 1, core, 1 : rows + 1] = stage[0, chip]

    pl.semaphore_wait(
        barrier, chips + has_low.astype(jnp.int32) + has_high.astype(jnp.int32)
    )

    def main_copy(conv, d):
        q = peer(d)
        return remote(
            stage.at[conv, q], act.at[conv, chip + 1, core, pl.ds(1, rows)],
            ms_sem.at[conv, d], mr_sem.at[conv, d], q * 2 + core, z,
        )

    def past_up(conv):
        return remote(
            act.at[conv, 0, :, rows], act.at[conv, 0, :, 0],
            qs_sem.at[conv, 0], qr_sem.at[conv, 0], t, z + 1,
        )

    def past_down(conv):
        return remote(
            act.at[conv, 0, :, 1], act.at[conv, 0, :, rows + 1],
            qs_sem.at[conv, 1], qr_sem.at[conv, 1], t, z - 1,
        )

    def halo_up(conv):
        return remote(
            act.at[conv, pl.ds(1, chips), core, rows], act.at[conv, pl.ds(1, chips), core, 0],
            hs_sem.at[conv, 0], hr_sem.at[conv, 0], t, z + 1,
        )

    def halo_down(conv):
        return remote(
            act.at[conv, pl.ds(1, chips), core, 1],
            act.at[conv, pl.ds(1, chips), core, rows + 1],
            hs_sem.at[conv, 1], hr_sem.at[conv, 1], t, z - 1,
        )

    def give_main(conv, whose):
        part = act.at[conv, pl.ds(1, chips), whose, pl.ds(1, rows)]
        return remote(part, part, fs_sem.at[conv], fr_sem.at[conv], mate, z)

    def give_halo(conv, side, whose):
        part = act.at[conv, pl.ds(1, chips), whose, side * (rows + 1)]
        return remote(part, part, gs_sem.at[conv, side], gr_sem.at[conv, side], mate, z)

    def part_copy(conv, d):
        return remote(
            psend.at[conv, d - 1], precv.at[conv, d - 1],
            ps_sem.at[conv, d - 1], pr_sem.at[conv, d - 1], peer(d) * 2 + core, z,
        )

    def exchange(conv):
        for d in range(1, chips):
            main_copy(conv, d).start()
        if conv == 0:
            sent_weight(0, w1).start()
            for c in (0, 1):

                @pl.when(has_high)
                def _():
                    past_up(c).start()

                @pl.when(has_low)
                def _():
                    past_down(c).start()

        for d in range(1, chips):
            remote(
                stage.at[conv, 0],
                act.at[conv, lax.rem(chip + chips - d, chips) + 1, core, pl.ds(1, rows)],
                ms_sem.at[conv, d], mr_sem.at[conv, d], mate, z,
            ).wait_recv()

        @pl.when(has_high)
        def _():
            halo_up(conv).start()

        @pl.when(has_low)
        def _():
            halo_down(conv).start()

        give_main(conv, core).start()

        @pl.when(has_low)
        def _():
            halo_up(conv).wait_recv()
            give_halo(conv, 0, core).start()

        @pl.when(has_high)
        def _():
            halo_down(conv).wait_recv()
            give_halo(conv, 1, core).start()

        @pl.when(has_low)
        def _():
            past_up(conv).wait_recv()
            give_halo(conv, 0, 1 - core).wait_recv()

        @pl.when(has_high)
        def _():
            past_down(conv).wait_recv()
            give_halo(conv, 1, 1 - core).wait_recv()

        give_main(conv, 1 - core).wait_recv()

    def convolve(conv):
        def shift(n, _):
            flat = act[conv, n // 2, n % 2].reshape((rows + 2) * wide, LANES).astype(F32)
            size = (rows + 2) * wide
            shifted[0, n] = pltpu.roll(flat, 1, 0).astype(BF).reshape(rows + 2, wide, LANES)
            shifted[1, n] = pltpu.roll(flat, size - 1, 0).astype(BF).reshape(rows + 2, wide, LANES)
            return 0

        lax.fori_loop(0, 2 * (chips + 1), shift, 0)

        def frame(q):
            acc = jnp.zeros((rows * wide, chans), F32)
            for tap in range(3):
                n = 2 * q + core + tap
                pieces = []
                for r in range(3):
                    pieces.append(shifted[0, n, r : r + rows].reshape(rows * wide, LANES))
                    pieces.append(act[conv, n // 2, n % 2, r : r + rows].reshape(rows * wide, LANES))
                    pieces.append(shifted[1, n, r : r + rows].reshape(rows * wide, LANES))
                acc = acc + jnp.dot(
                    jnp.concatenate(pieces, axis=1),
                    weights[conv, 9 * tap : 9 * tap + 9].reshape(9 * LANES, chans),
                    preferred_element_type=F32,
                )
            return acc.reshape(rows, wide, chans)[:, :cols].reshape(cells, chans)

        def step(d, _):
            psend[conv, d - 1] = frame(peer(d)).astype(BF)
            part_copy(conv, d).start()
            return 0

        lax.fori_loop(1, chips, step, 0)
        own[...] = frame(chip)
        for d in range(1, chips):
            part_copy(conv, d).wait_recv()
            own[...] += precv[conv, d - 1].astype(F32)
        return own[...]

    exchange(0)
    sent_weight(1, w2).start()
    local_weight(0, w1).wait()
    remote(w1, weights.at[0, :, 1 - core], ws_sem.at[0], wr_sem.at[0], mate, z).wait_recv()
    hidden = convolve(0) + bias1[...]
    put_stage(1, silu(normalize(hidden, gain2[...])))
    act[1, chip + 1, core, 1 : rows + 1] = stage[1, chip]
    exchange(1)
    local_weight(1, w2).wait()
    remote(w2, weights.at[1, :, 1 - core], ws_sem.at[1], wr_sem.at[1], mate, z).wait_recv()
    block = (video[...].astype(F32) + (convolve(1) + bias2[...])).astype(BF)
    out[...] = block
    held[z] = normalize(block.astype(F32), gain3[...]).astype(BF)

    def right(b):
        return remote(held.at[b], held.at[b], xright_sem.at[b], xr_sem.at[b], t, z + 1)

    def left(b):
        return remote(held.at[b], held.at[b], xleft_sem.at[b], xr_sem.at[b], t, z - 1)

    @pl.when(has_high)
    def _():
        right(z).start()

    @pl.when(has_low)
    def _():
        left(z).start()

    factor = 1.0 / (float(chans) ** 0.5)
    queries[...] = jnp.dot(held[z], wq[...], preferred_element_type=F32).astype(BF)
    top[...] = jnp.full(top.shape, -jnp.inf, F32)
    total[...] = jnp.zeros(total.shape, F32)
    accum[...] = jnp.zeros(accum.shape, F32)

    def attend(b):
        tokens = held[b]
        keys = jnp.dot(tokens, wk[...], preferred_element_type=F32).astype(BF)
        values = jnp.dot(tokens, wv[...], preferred_element_type=F32).astype(BF)
        scores = lax.dot_general(
            queries[...], keys, (((1,), (1,)), ((), ())), preferred_element_type=F32
        ) * factor
        before = top[...]
        now = jnp.maximum(before, jnp.max(scores, axis=1, keepdims=True))
        shrink = jnp.exp(before - now)
        expo = jnp.exp(scores - now)
        top[...] = now
        total[...] = total[...] * shrink + jnp.sum(expo, axis=1, keepdims=True)
        accum[...] = accum[...] * shrink + jnp.dot(
            expo.astype(BF), values, preferred_element_type=F32
        )

    attend(z)

    def ring(k, _):
        @pl.when(z - k >= 0)
        def _():
            left_band = z - k
            right(left_band).wait_recv()

            @pl.when(has_high)
            def _():
                right(left_band).start()

        @pl.when(z + k < bands)
        def _():
            right_band = z + k
            left(right_band).wait_recv()

            @pl.when(has_low)
            def _():
                left(right_band).start()

        @pl.when(z - k >= 0)
        def _():
            attend(z - k)

        @pl.when(z + k < bands)
        def _():
            attend(z + k)

        return 0

    lax.fori_loop(1, bands, ring, 0)
    att = (accum[...] / total[...]).astype(BF)
    out[...] = (
        out[...].astype(F32) + jnp.dot(att, wo[...], preferred_element_type=F32)
    ).astype(BF)

    def drain(b, _):
        @pl.when(jnp.logical_and(has_high, b <= z))
        def _():
            right(b).wait_send()

        @pl.when(jnp.logical_and(has_low, b >= z))
        def _():
            left(b).wait_send()

        return 0

    lax.fori_loop(0, bands, drain, 0)
    for conv, w in ((0, w1), (1, w2)):
        sent_weight(conv, w).wait_send()
        give_main(conv, core).wait_send()
        for d in range(1, chips):
            main_copy(conv, d).wait_send()
            part_copy(conv, d).wait_send()

        @pl.when(has_high)
        def _():
            halo_up(conv).wait_send()
            past_up(conv).wait_send()
            give_halo(conv, 1, core).wait_send()

        @pl.when(has_low)
        def _():
            halo_down(conv).wait_send()
            past_down(conv).wait_send()
            give_halo(conv, 0, core).wait_send()


def local(
    devices, bands,
    video, past_first, past_second, conv_first, bias_first, conv_second, bias_second,
    gain_first, gain_second, gain_attn, query_weight, key_weight, value_weight, out_weight,
):
    _, rows, cols, chans = video.shape
    chips = devices // 2
    share = chans // devices
    wide = (cols + 1 + 15) // 16 * 16
    cells = rows * cols
    chip = lax.axis_index("tm") // 2

    def past_part(past):
        part = lax.dynamic_slice_in_dim(past, chip * 2 * share, 2 * share, axis=3)
        part = part.reshape(2, rows, cols, 2, share)
        part = jnp.pad(part, ((0, 0), (0, 0), (0, wide - cols), (0, 0), (0, SLOT - share)))
        return part.reshape(2, rows, wide, LANES)

    def weight_part(kernel_piece):
        flat = kernel_piece.reshape(27, share, chans)
        return jnp.pad(flat, ((0, 0), (0, SLOT - share), (0, 0)))

    channel = jnp.arange(chans)
    place = (channel // share) * SLOT + channel % share
    select = (place[:, None] == jnp.arange(chips * LANES)[None, :]).astype(BF)

    vmem = pl.BlockSpec(memory_space=pltpu.VMEM)
    hbm = pl.BlockSpec(memory_space=pl.ANY)
    dma = pltpu.SemaphoreType.DMA
    flops = 2 * 2 * cells * 27 * chans * chans + 4 * cells * cells * bands * chans
    row = lambda v: v.reshape(1, chans)
    encoded = pl.pallas_call(
        functools.partial(kernel, chips, bands, rows, cols, wide),
        out_shape=jax.ShapeDtypeStruct((cells, chans), BF),
        in_specs=[vmem] * 3 + [hbm] * 2 + [vmem] * 10,
        out_specs=vmem,
        scratch_shapes=[
            pltpu.VMEM((2, 27, 2, SLOT, chans), BF),
            pltpu.VMEM((2, chips, rows, wide, LANES), BF),
            pltpu.VMEM((2, chips + 1, 2, rows + 2, wide, LANES), BF),
            pltpu.VMEM((2, 2 * (chips + 1), rows + 2, wide, LANES), BF),
            pltpu.VMEM((2, chips - 1, cells, chans), BF),
            pltpu.VMEM((2, chips - 1, cells, chans), BF),
            pltpu.VMEM((cells, chans), F32),
            pltpu.VMEM((bands, cells, chans), BF),
            pltpu.VMEM((cells, chans), BF),
            pltpu.VMEM((cells, 1), F32),
            pltpu.VMEM((cells, 1), F32),
            pltpu.VMEM((cells, chans), F32),
            dma((2,)), dma((2,)), dma((2,)),
            dma((2, chips)), dma((2, chips)),
            dma((2, 2)), dma((2, 2)), dma((2, 2)), dma((2, 2)),
            dma((2,)), dma((2,)), dma((2, 2)), dma((2, 2)),
            dma((2, chips)), dma((2, chips)),
            dma((bands,)), dma((bands,)), dma((bands,)),
        ],
        compiler_params=pltpu.CompilerParams(
            collective_id=0, has_side_effects=True, vmem_limit_bytes=56 * 1024 * 1024
        ),
        cost_estimate=pl.CostEstimate(
            flops=flops, bytes_accessed=8 * 1024 * 1024, transcendentals=cells * cells * bands
        ),
    )(
        video.reshape(cells, chans), past_part(past_first), past_part(past_second),
        weight_part(conv_first), weight_part(conv_second),
        row(bias_first), row(bias_second), row(gain_first), row(gain_second), row(gain_attn),
        select, query_weight, key_weight, value_weight, out_weight,
    )
    return encoded.reshape(video.shape)


def solution(mesh):
    return jax.shard_map(
        functools.partial(local, mesh.shape["tm"], mesh.shape["band"]),
        mesh=mesh,
        in_specs=(
            P("tm", "band", None, None),
            P(None, "band", None, None),
            P(None, "band", None, None),
            P(None, None, None, "tm", None),
            P(),
            P(None, None, None, "tm", None),
            P(),
            P(),
            P(),
            P(),
            P(),
            P(),
            P(),
            P(),
        ),
        out_specs=P("tm", "band", None, None),
        check_vma=False,
    )
```

time: 249 us -> 113 us (0.45)
  waiting for transfers between devices: 123 us -> 0 us
  Pallas kernels: 0 us -> 98.1 us
  starting transfers between devices: 30.9 us -> 0 us
  matrix products: 27.9 us -> 0 us
  local copies, waits for them, and re-layouts: 39.2 us -> 14 us
  between operations: 13.4 us -> 0.06 us
  other arithmetic: 13.9 us -> 0.91 us
    pallas_call x0 -> x1, Pallas kernels: none -> 98.1 us  [local(): pl.pallas_call(functools.partial(kernel, chips, bands, rows, cols, wide),...]
    all_gather x4 -> x0, waiting for transfers between devices: 78 us -> none  [the longest x1 43 us: local(): lax.all_gather(key_rows, 'band', axis=0, tiled=True)]
    ppermute x8 -> x0, waiting for transfers between devices: 43.9 us -> none  [the longest x4 29.3 us: from_behind(): return lax.ppermute(x, axis, pairs)]
    unnamed x70 -> x7, local copies, waits for them, and re-layouts: 37.4 us -> 2.03 us
    ppermute x8 -> x0, starting transfers between devices: 30.8 us -> none  [the longest x4 19.9 us: from_behind(): return lax.ppermute(x, axis, pairs)]
    dot_general x6 -> x0, matrix products: 27.9 us -> none  [the longest x2 19.7 us: convolve(): summed = jnp.dot(columns, flat, preferred_element_type=jnp.float32)]
    reshape x0 -> x7, local copies, waits for them, and re-layouts: none -> 7.99 us  [the longest x5 6.32 us: local(): row = lambda v: v.reshape(1, chans)]
    unnamed x6 -> x0, other arithmetic: 5.2 us -> none
  transfers between devices with their start and end apart: 12 -> 0, of which waited for: 9 -> 0; matrix products, arithmetic and copies ran while one was open for 27% -> 0% of each run, Pallas kernels for 0% -> 0%
where the time goes in v1:
time: 113 us
  Pallas kernels  98.1 us (87%)
  local copies, waits for them, and re-layouts  14 us (12%)
    pallas_call x1, Pallas kernels, local(): pl.pallas_call(functools.partial(kernel, chips, bands, rows, cols, wide),...  98.1 us
    reshape x5, local copies, waits for them, and re-layouts, local(): row = lambda v: v.reshape(1, chans)  6.32 us
    pad x2, local copies, waits for them, and re-layouts, weight_part(): return jnp.pad(flat, ((0, 0), (0, SLOT - share), (0, 0)))  2.57 us

profile of v1, /device:TPU:0, one launch (start us, length us, event | category | flops | bytes accessed | tf_op | source)
XLA Modules:
  0.0 113.1 jit_solution(836970366207531486)
XLA Ops:
  0.0 1.3 %reshape.65.bias1 = f32[1,384]{1,0:T(1,128)} reshape(f32[384]{0:T(512)} %param.18) | data formatting | bytes 3072 | tf_op jit(solution)/shard_map/reshape | solution.py:391
  1.3 1.3 %reshape.66.bias2 = f32[1,384]{1,0:T(1,128)} reshape(f32[384]{0:T(512)} %param.20) | data formatting | bytes 3072 | tf_op jit(solution)/shard_map/reshape | solution.py:391
  2.5 1.3 %reshape.67.gain1 = f32[1,384]{1,0:T(1,128)} reshape(f32[384]{0:T(512)} %param.21) | data formatting | bytes 3072 | tf_op jit(solution)/shard_map/reshape | solution.py:391
  3.8 1.3 %reshape.68.gain2 = f32[1,384]{1,0:T(1,128)} reshape(f32[384]{0:T(512)} %param.22) | data formatting | bytes 3072 | tf_op jit(solution)/shard_map/reshape | solution.py:391
  5.1 1.2 %reshape.69.gain3 = f32[1,384]{1,0:T(1,128)} reshape(f32[384]{0:T(512)} %param.23) | data formatting | bytes 3072 | tf_op jit(solution)/shard_map/reshape | solution.py:391
  6.3 0.9 fusion.select
  7.2 1.3 %constant_dynamic-slice_fusion = (bf16[2,4,104,96]{3,2,1,0:T(8,128)(2,1)S(1)}, bf16[2,4,104,96]{3,2,1,0:T(8,128)(2,1)S(1)}) fusion(bf16[2,4,104,384]{3,2,1,0:T(8,128)(2,1)} %param.16, s32[]{:T(128)S(6)} %select_n.29, bf16[2,4,104,384]{3,2,1,0:T(8,128)(2,1)} %param.15), kind=kLoop, calls=%fused_computation.15 | loop fusion | bytes 638980 | tf_op jit(solution)/shard_map/dynamic_slice | solution.py:374
  8.6 0.0 copy-start
  8.6 0.1 copy.20
  8.7 0.1 pad.15
  8.8 0.8 copy.18.past2
  9.6 0.1 copy.19
  9.8 0.1 pad.14
  9.9 0.0 copy-start.1
  9.9 0.8 copy.17.past1
  10.7 0.0 copy-done
  10.7 1.3 %pad.16.w1 = bf16[27,64,384]{2,1,0:T(8,128)(2,1)} pad(bf16[27,48,384]{2,1,0:T(8,128)(2,1)S(1)} %bitcast.10, bf16[]{:T(256)} %constant.43.clone.1), padding=0_0x0_16x0_0 | pad | bytes 2322434 | tf_op jit(solution)/shard_map/jit(_pad)/pad | solution.py:381
  12.0 0.0 copy-done.1
  12.0 1.3 %pad.17.w2 = bf16[27,64,384]{2,1,0:T(8,128)(2,1)} pad(bf16[27,48,384]{2,1,0:T(8,128)(2,1)S(1)} %bitcast.11, bf16[]{:T(256)} %constant.43.clone.1), padding=0_0x0_16x0_0 | pad | bytes 2322434 | tf_op jit(solution)/shard_map/jit(_pad)/pad | solution.py:381
  13.3 98.1 %shard_map.136 = bf16[416,384]{1,0:T(8,128)(2,1)} custom-call(bf16[416,384]{1,0:T(8,128)(2,1)} %bitcast.15, bf16[2,4,112,128]{3,2,1,0:T(8,128)(2,1)} %copy.17.past1, bf16[2,4,112,128]{3,2,1,0:T(8,128)(2,1)} %copy.18.past2, bf16[27,64,384]{2,1,0:T(8,128)(2,1)} %pad.16.w1, bf16[27,64,384]{2,1,0:T(8,128)(2,1)} %pad.17.w2, f32[1,384]{1,0:T(1,128)} %reshape.65.bias1, ...), custom_call_target="tpu_custom_call" | custom-call | flops 7688159232 | bytes 8388608 | tf_op jit(solution)/shard_map/pallas_call | solution.py:392
  111.4 1.7 %copy.22 = bf16[1,4,104,384]{3,2,1,0:T(8,128)(2,1)} copy(bf16[1,4,104,384]{3,2,1,0:T(8,128)(2,1)} %bitcast.14) | data formatting | bytes 638976
  (1 shorter events, 0.0 us)
Async XLA Ops:
  8.6 2.1 %copy-start = (bf16[3,3,3,48,384]{4,3,2,1,0:T(8,128)(2,1)S(1)}, bf16[3,3,3,48,384]{4,3,2,1,0:T(8,128)(2,1)}, u32[]{:S(2)}) copy-start(bf16[3,3,3,48,384]{4,3,2,1,0:T(8,128)(2,1)} %param.17) | copy-start | bytes 2985988
  9.9 2.1 %copy-start.1 = (bf16[3,3,3,48,384]{4,3,2,1,0:T(8,128)(2,1)S(1)}, bf16[3,3,3,48,384]{4,3,2,1,0:T(8,128)(2,1)}, u32[]{:S(2)}) copy-start(bf16[3,3,3,48,384]{4,3,2,1,0:T(8,128)(2,1)} %param.19) | copy-start | bytes 2985988

commit v2 on v1

--- a/solution.py
+++ b/solution.py
@@ -24,9 +24,10 @@
 
 def kernel(
     chips, bands, rows, cols, wide,
-    video, past1, past2, w1, w2, bias1, bias2, gain1, gain2, gain3, select,
+    share, direct,
+    video, past1, past2, w1, w2, bias1, bias2, gain1, gain2, gain3,
     wq, wk, wv, wo, out,
-    weights, stage, act, shifted, psend, precv, own, held, queries, top, total, accum,
+    weights, stage, act, shifted, psend, precv, work, kept, held, queries, top, total, accum,
     wl_sem, ws_sem, wr_sem, ms_sem, mr_sem, hs_sem, hr_sem, qs_sem, qr_sem,
     fs_sem, fr_sem, gs_sem, gr_sem, ps_sem, pr_sem, xr_sem, xright_sem, xleft_sem,
 ):
@@ -36,7 +37,9 @@
     core = t % 2
     mate = t + 1 - 2 * core
     last = bands - 1
+    plane = chips == 4 and rows % 4 == 0
     cells = rows * cols
+    half = rows // 2
     chans = video.shape[1]
     has_low = z > 0
     has_high = z < last
@@ -63,48 +66,81 @@
     def _():
         pl.semaphore_signal(barrier, inc=1, device_id=(t, z + 1), device_id_type=MESH)
 
+    def weight_slot(conv, whose):
+        slot = weights.at[conv, :, whose]
+        return slot.at[:, pl.ds(0, share)] if direct else slot
+
     def local_weight(conv, w):
-        return pltpu.make_async_copy(w, weights.at[conv, :, core], wl_sem.at[conv])
+        return pltpu.make_async_copy(w, weight_slot(conv, core), wl_sem.at[conv])
 
     def sent_weight(conv, w):
         return remote(
-            w, weights.at[conv, :, core], ws_sem.at[conv], wr_sem.at[conv], mate, z
-        )
-
-    def put_stage(conv, values):
-        cube = values.reshape(rows, cols, chans)
-        cube = jnp.concatenate([cube, jnp.zeros((rows, wide - cols, chans), F32)], axis=1)
-        flat = cube.reshape(rows * wide, chans).astype(BF)
-        spread = jnp.dot(flat, select[...], preferred_element_type=F32).astype(BF)
+            w, weight_slot(conv, core), ws_sem.at[conv], wr_sem.at[conv], mate, z
+        )
+
+    def spread_of(values, first, count):
+        lead = values.shape[0] // cols
+        cube = values.reshape(lead, cols, chans)
+        cube = jnp.concatenate([cube, jnp.zeros((lead, wide - cols, chans), F32)], axis=1)
+        flat = cube.reshape(lead * wide, chans).astype(BF)
+        channel = lax.broadcasted_iota(jnp.int32, (chans, count * LANES), 0)
+        lane = lax.broadcasted_iota(jnp.int32, (chans, count * LANES), 1)
+        within = lane % SLOT
+        source = (lane // SLOT + 2 * first) * share + within
+        chosen = jnp.logical_and(channel == source, within < share)
+        select = jnp.where(chosen, 1.0, 0.0).astype(BF)
+        return jnp.dot(flat, select, preferred_element_type=F32).astype(BF)
+
+    def put_stage(conv, h, values):
+        spread = spread_of(values, 0, chips)
+        mine = pl.ds(h * half, half)
         for q in range(chips):
-            stage[conv, q] = spread[:, q * LANES : (q + 1) * LANES].reshape(rows, wide, LANES)
-
-    for conv, past in ((0, past1), (1, past2)):
-        act[conv, 0, :, 1 : rows + 1] = past[...]
-
-        @pl.when(z == 0)
-        def _():
-            act[conv, :, :, 0:1] = jnp.zeros((chips + 1, 2, 1, wide, LANES), BF)
-
-        @pl.when(z == last)
-        def _():
-            act[conv, :, :, rows + 1 : rows + 2] = jnp.zeros((chips + 1, 2, 1, wide, LANES), BF)
+            stage[conv, q, mine] = spread[:, q * LANES : (q + 1) * LANES].reshape(
+                half, wide, LANES
+            )
+        act[conv, chip + 1, core, pl.ds(1 + h * half, half)] = stage[conv, chip, mine]
+
+    def fill_past():
+        for conv, past in ((0, past1), (1, past2)):
+            for n in range(2):
+                part = spread_of(past[n].reshape(cells, chans).astype(F32), chip, 1)
+                act[conv, 0, n, 1 : rows + 1] = part.reshape(rows, wide, LANES)
+            if direct:
+                weights[conv, :, :, share:] = jnp.zeros((27, 2, SLOT - share, chans), BF)
+
+            @pl.when(z == 0)
+            def _():
+                act[conv, :, :, 0:1] = jnp.zeros((chips + 1, 2, 1, wide, LANES), BF)
+
+            @pl.when(z == last)
+            def _():
+                act[conv, :, :, rows + 1 : rows + 2] = jnp.zeros((chips + 1, 2, 1, wide, LANES), BF)
 
     local_weight(0, w1).start()
     local_weight(1, w2).start()
     vid = video[...].astype(F32)
-    put_stage(0, silu(normalize(vid, gain1[...])))
-    act[0, chip + 1, core, 1 : rows + 1] = stage[0, chip]
+    active = silu(normalize(vid, gain1[...].reshape(1, chans)))
+    for h in range(2):
+        put_stage(0, h, active[h * half * cols : (h + 1) * half * cols])
 
     pl.semaphore_wait(
         barrier, chips + has_low.astype(jnp.int32) + has_high.astype(jnp.int32)
     )
 
-    def main_copy(conv, d):
+    def main_copy(conv, d, h):
         q = peer(d)
         return remote(
-            stage.at[conv, q], act.at[conv, chip + 1, core, pl.ds(1, rows)],
-            ms_sem.at[conv, d], mr_sem.at[conv, d], q * 2 + core, z,
+            stage.at[conv, q, pl.ds(h * half, half)],
+            act.at[conv, chip + 1, core, pl.ds(1 + h * half, half)],
+            ms_sem.at[conv, d, h], mr_sem.at[conv, d, h], q * 2 + core, z,
+        )
+
+    def main_came(conv, d, h):
+        source = lax.rem(chip + chips - d, chips)
+        return remote(
+            stage.at[conv, 0, pl.ds(h * half, half)],
+            act.at[conv, source + 1, core, pl.ds(1 + h * half, half)],
+            ms_sem.at[conv, d, h], mr_sem.at[conv, d, h], mate, z,
         )
 
     def past_up(conv):
@@ -143,14 +179,27 @@
     def part_copy(conv, d):
         return remote(
             psend.at[conv, d - 1], precv.at[conv, d - 1],
-            ps_sem.at[conv, d - 1], pr_sem.at[conv, d - 1], peer(d) * 2 + core, z,
+            ps_sem.at[conv, d - 1, 0], pr_sem.at[conv, d - 1, 0], peer(d) * 2 + core, z,
+        )
+
+    across = chip + 1 - 2 * (chip % 2)
+    along = chip + 2 - 4 * (chip // 2)
+
+    def row_copy(conv, kind, r):
+        first, second = (across, along) if r % 2 == 0 else (along, across)
+        target = second if kind == 2 else first
+        return remote(
+            psend.at[conv, kind, r], precv.at[conv, kind, r],
+            ps_sem.at[conv, kind, r], pr_sem.at[conv, kind, r], target * 2 + core, z,
         )
 
     def exchange(conv):
-        for d in range(1, chips):
-            main_copy(conv, d).start()
         if conv == 0:
             sent_weight(0, w1).start()
+            for h in range(2):
+                for d in range(1, chips):
+                    main_copy(conv, d, h).start()
+            fill_past()
             for c in (0, 1):
 
                 @pl.when(has_high)
@@ -162,19 +211,18 @@
                     past_down(c).start()
 
         for d in range(1, chips):
-            remote(
-                stage.at[conv, 0],
-                act.at[conv, lax.rem(chip + chips - d, chips) + 1, core, pl.ds(1, rows)],
-                ms_sem.at[conv, d], mr_sem.at[conv, d], mate, z,
-            ).wait_recv()
+            main_came(conv, d, 0).wait_recv()
+
+        @pl.when(has_low)
+        def _():
+            halo_down(conv).start()
+
+        for d in range(1, chips):
+            main_came(conv, d, 1).wait_recv()
 
         @pl.when(has_high)
         def _():
             halo_up(conv).start()
-
-        @pl.when(has_low)
-        def _():
-            halo_down(conv).start()
 
         give_main(conv, core).start()
 
@@ -200,7 +248,7 @@
 
         give_main(conv, 1 - core).wait_recv()
 
-    def convolve(conv):
+    def convolve(conv, consume):
         def shift(n, _):
             flat = act[conv, n // 2, n % 2].reshape((rows + 2) * wide, LANES).astype(F32)
             size = (rows + 2) * wide
@@ -224,56 +272,120 @@
                     weights[conv, 9 * tap : 9 * tap + 9].reshape(9 * LANES, chans),
                     preferred_element_type=F32,
                 )
-            return acc.reshape(rows, wide, chans)[:, :cols].reshape(cells, chans)
+            work[...] = acc.reshape(rows, wide, chans)[:, :cols]
+
+        def sum_row(r):
+            row_copy(conv, 0, r).wait_recv()
+            psend[conv, 2, r] = (kept[r] + precv[conv, 0, r].astype(F32)).astype(BF)
+            row_copy(conv, 2, r).start()
+
+        def plane_step(i, _):
+            x = (chip + 1 - i // 2) % 2
+            y = (chip // 2 + 1 - i % 2) % 2
+            frame(2 * y + x)
+
+            @pl.when(i == 0)
+            def _():
+                for r in range(rows):
+                    psend[conv, 0, r] = work[r].astype(BF)
+                    row_copy(conv, 0, r).start()
+
+            @pl.when(i == 1)
+            def _():
+                for r in range(0, rows, 2):
+                    psend[conv, 1, r] = work[r].astype(BF)
+                    if r < half:
+                        row_copy(conv, 1, r).start()
+                    kept[r + 1] = work[r + 1]
+
+            @pl.when(i == 2)
+            def _():
+                for r in range(0, rows, 2):
+                    psend[conv, 1, r + 1] = work[r + 1].astype(BF)
+                    if r + 1 < half:
+                        row_copy(conv, 1, r + 1).start()
+                    kept[r] = work[r]
+                for r in range(half):
+                    sum_row(r)
+                for r in range(half, rows):
+                    row_copy(conv, 1, r).start()
+
+            return 0
 
         def step(d, _):
-            psend[conv, d - 1] = frame(peer(d)).astype(BF)
+            frame(peer(d))
+            psend[conv, d - 1] = work[...].astype(BF)
             part_copy(conv, d).start()
             return 0
 
-        lax.fori_loop(1, chips, step, 0)
-        own[...] = frame(chip)
-        for d in range(1, chips):
-            part_copy(conv, d).wait_recv()
-            own[...] += precv[conv, d - 1].astype(F32)
-        return own[...]
+        if plane:
+            lax.fori_loop(0, 4, plane_step, 0)
+            for r in range(half, rows):
+                sum_row(r)
+        else:
+            lax.fori_loop(1, chips, step, 0)
+            frame(chip)
+            for d in range(1, chips):
+                part_copy(conv, d).wait_recv()
+        for h in range(2):
+            mine = slice(h * half, (h + 1) * half)
+            for kind in range(1 if plane else 0, chips - 1):
+                if plane:
+                    for r in range(h * half, (h + 1) * half):
+                        row_copy(conv, kind, r).wait_recv()
+                work[mine] += precv[conv, kind, mine].astype(F32)
+            consume(h, work[mine].reshape(half * cols, chans))
 
     exchange(0)
     sent_weight(1, w2).start()
     local_weight(0, w1).wait()
-    remote(w1, weights.at[0, :, 1 - core], ws_sem.at[0], wr_sem.at[0], mate, z).wait_recv()
-    hidden = convolve(0) + bias1[...]
-    put_stage(1, silu(normalize(hidden, gain2[...])))
-    act[1, chip + 1, core, 1 : rows + 1] = stage[1, chip]
+    remote(w1, weight_slot(0, 1 - core), ws_sem.at[0], wr_sem.at[0], mate, z).wait_recv()
+
+    def after_first(h, summed):
+        hidden = summed + bias1[...].reshape(1, chans)
+        put_stage(1, h, silu(normalize(hidden, gain2[...].reshape(1, chans))))
+        for d in range(1, chips):
+            main_copy(1, d, h).start()
+
+    convolve(0, after_first)
     exchange(1)
     local_weight(1, w2).wait()
-    remote(w2, weights.at[1, :, 1 - core], ws_sem.at[1], wr_sem.at[1], mate, z).wait_recv()
-    block = (video[...].astype(F32) + (convolve(1) + bias2[...])).astype(BF)
-    out[...] = block
-    held[z] = normalize(block.astype(F32), gain3[...]).astype(BF)
-
-    def right(b):
-        return remote(held.at[b], held.at[b], xright_sem.at[b], xr_sem.at[b], t, z + 1)
-
-    def left(b):
-        return remote(held.at[b], held.at[b], xleft_sem.at[b], xr_sem.at[b], t, z - 1)
-
-    @pl.when(has_high)
-    def _():
-        right(z).start()
-
-    @pl.when(has_low)
-    def _():
-        left(z).start()
-
+    remote(w2, weight_slot(1, 1 - core), ws_sem.at[1], wr_sem.at[1], mate, z).wait_recv()
+
+    def right(b, h):
+        return remote(
+            held.at[b, h], held.at[b, h], xright_sem.at[b, h], xr_sem.at[b, h], t, z + 1
+        )
+
+    def left(b, h):
+        return remote(
+            held.at[b, h], held.at[b, h], xleft_sem.at[b, h], xr_sem.at[b, h], t, z - 1
+        )
+
+    def after_second(h, summed):
+        mine = slice(h * half * cols, (h + 1) * half * cols)
+        conv_out = summed + bias2[...].reshape(1, chans)
+        block = (video[mine].astype(F32) + conv_out).astype(BF)
+        out[mine] = block
+        held[z, h] = normalize(block.astype(F32), gain3[...].reshape(1, chans)).astype(BF)
+
+        @pl.when(has_high)
+        def _():
+            right(z, h).start()
+
+        @pl.when(has_low)
+        def _():
+            left(z, h).start()
+
+    convolve(1, after_second)
     factor = 1.0 / (float(chans) ** 0.5)
-    queries[...] = jnp.dot(held[z], wq[...], preferred_element_type=F32).astype(BF)
+    queries[...] = jnp.dot(held[z].reshape(cells, chans), wq[...], preferred_element_type=F32).astype(BF)
     top[...] = jnp.full(top.shape, -jnp.inf, F32)
     total[...] = jnp.zeros(total.shape, F32)
     accum[...] = jnp.zeros(accum.shape, F32)
 
     def attend(b):
-        tokens = held[b]
+        tokens = held[b].reshape(cells, chans)
         keys = jnp.dot(tokens, wk[...], preferred_element_type=F32).astype(BF)
         values = jnp.dot(tokens, wv[...], preferred_element_type=F32).astype(BF)
         scores = lax.dot_general(
@@ -292,23 +404,23 @@
     attend(z)
 
     def ring(k, _):
-        @pl.when(z - k >= 0)
-        def _():
-            left_band = z - k
-            right(left_band).wait_recv()
-
-            @pl.when(has_high)
-            def _():
-                right(left_band).start()
-
-        @pl.when(z + k < bands)
-        def _():
-            right_band = z + k
-            left(right_band).wait_recv()
-
-            @pl.when(has_low)
-            def _():
-                left(right_band).start()
+        for h in range(2):
+
+            @pl.when(z - k >= 0)
+            def _():
+                right(z - k, h).wait_recv()
+
+                @pl.when(has_high)
+                def _():
+                    right(z - k, h).start()
+
+            @pl.when(z + k < bands)
+            def _():
+                left(z + k, h).wait_recv()
+
+                @pl.when(has_low)
+                def _():
+                    left(z + k, h).start()
 
         @pl.when(z - k >= 0)
         def _():
@@ -329,11 +441,13 @@
     def drain(b, _):
         @pl.when(jnp.logical_and(has_high, b <= z))
         def _():
-            right(b).wait_send()
+            for h in range(2):
+                right(b, h).wait_send()
 
         @pl.when(jnp.logical_and(has_low, b >= z))
         def _():
-            left(b).wait_send()
+            for h in range(2):
+                left(b, h).wait_send()
 
         return 0
 
@@ -342,8 +456,13 @@
         sent_weight(conv, w).wait_send()
         give_main(conv, core).wait_send()
         for d in range(1, chips):
-            main_copy(conv, d).wait_send()
-            part_copy(conv, d).wait_send()
+            for h in range(2):
+                main_copy(conv, d, h).wait_send()
+            if plane:
+                for r in range(rows):
+                    row_copy(conv, d - 1, r).wait_send()
+            else:
+                part_copy(conv, d).wait_send()
 
         @pl.when(has_high)
         def _():
@@ -368,51 +487,43 @@
     share = chans // devices
     wide = (cols + 1 + 15) // 16 * 16
     cells = rows * cols
-    chip = lax.axis_index("tm") // 2
-
-    def past_part(past):
-        part = lax.dynamic_slice_in_dim(past, chip * 2 * share, 2 * share, axis=3)
-        part = part.reshape(2, rows, cols, 2, share)
-        part = jnp.pad(part, ((0, 0), (0, 0), (0, wide - cols), (0, 0), (0, SLOT - share)))
-        return part.reshape(2, rows, wide, LANES)
+    direct = share % 16 == 0 and share < SLOT
 
     def weight_part(kernel_piece):
         flat = kernel_piece.reshape(27, share, chans)
+        if direct:
+            return flat
         return jnp.pad(flat, ((0, 0), (0, SLOT - share), (0, 0)))
-
-    channel = jnp.arange(chans)
-    place = (channel // share) * SLOT + channel % share
-    select = (place[:, None] == jnp.arange(chips * LANES)[None, :]).astype(BF)
 
     vmem = pl.BlockSpec(memory_space=pltpu.VMEM)
     hbm = pl.BlockSpec(memory_space=pl.ANY)
     dma = pltpu.SemaphoreType.DMA
     flops = 2 * 2 * cells * 27 * chans * chans + 4 * cells * cells * bands * chans
-    row = lambda v: v.reshape(1, chans)
     encoded = pl.pallas_call(
-        functools.partial(kernel, chips, bands, rows, cols, wide),
+        functools.partial(kernel, chips, bands, rows, cols, wide, share, direct),
         out_shape=jax.ShapeDtypeStruct((cells, chans), BF),
-        in_specs=[vmem] * 3 + [hbm] * 2 + [vmem] * 10,
+        in_specs=[vmem] * 3 + [hbm] * 2 + [vmem] * 9,
         out_specs=vmem,
         scratch_shapes=[
             pltpu.VMEM((2, 27, 2, SLOT, chans), BF),
             pltpu.VMEM((2, chips, rows, wide, LANES), BF),
             pltpu.VMEM((2, chips + 1, 2, rows + 2, wide, LANES), BF),
             pltpu.VMEM((2, 2 * (chips + 1), rows + 2, wide, LANES), BF),
-            pltpu.VMEM((2, chips - 1, cells, chans), BF),
-            pltpu.VMEM((2, chips - 1, cells, chans), BF),
-            pltpu.VMEM((cells, chans), F32),
-            pltpu.VMEM((bands, cells, chans), BF),
+            pltpu.VMEM((2, chips - 1, rows, cols, chans), BF),
+            pltpu.VMEM((2, chips - 1, rows, cols, chans), BF),
+            pltpu.VMEM((rows, cols, chans), F32),
+            pltpu.VMEM((rows, cols, chans), F32),
+            pltpu.VMEM((bands, 2, cells // 2, chans), BF),
             pltpu.VMEM((cells, chans), BF),
             pltpu.VMEM((cells, 1), F32),
             pltpu.VMEM((cells, 1), F32),
             pltpu.VMEM((cells, chans), F32),
             dma((2,)), dma((2,)), dma((2,)),
-            dma((2, chips)), dma((2, chips)),
+            dma((2, chips, 2)), dma((2, chips, 2)),
             dma((2, 2)), dma((2, 2)), dma((2, 2)), dma((2, 2)),
             dma((2,)), dma((2,)), dma((2, 2)), dma((2, 2)),
-            dma((2, chips)), dma((2, chips)),
-            dma((bands,)), dma((bands,)), dma((bands,)),
+            dma((2, chips, rows)), dma((2, chips, rows)),
+            dma((bands, 2)), dma((bands, 2)), dma((bands, 2)),
         ],
         compiler_params=pltpu.CompilerParams(
             collective_id=0, has_side_effects=True, vmem_limit_bytes=56 * 1024 * 1024
@@ -421,10 +532,10 @@
             flops=flops, bytes_accessed=8 * 1024 * 1024, transcendentals=cells * cells * bands
         ),
     )(
-        video.reshape(cells, chans), past_part(past_first), past_part(past_second),
+        video.reshape(cells, chans), past_first, past_second,
         weight_part(conv_first), weight_part(conv_second),
-        row(bias_first), row(bias_second), row(gain_first), row(gain_second), row(gain_attn),
-        select, query_weight, key_weight, value_weight, out_weight,
+        bias_first, bias_second, gain_first, gain_second, gain_attn,
+        query_weight, key_weight, value_weight, out_weight,
     )
     return encoded.reshape(video.shape)
 

time: 113 us -> 81.4 us (0.72)
  Pallas kernels: 98.1 us -> 79.5 us
  local copies, waits for them, and re-layouts: 14 us -> 1.72 us
    pallas_call x1, Pallas kernels: 98.1 us -> 79.5 us  [local(): pl.pallas_call(functools.partial(kernel, chips, bands, rows, cols, wide,...]
    reshape x7 -> x0, local copies, waits for them, and re-layouts: 7.99 us -> none  [the longest x5 6.32 us: local(): row = lambda v: v.reshape(1, chans)]
    pad x4 -> x0, local copies, waits for them, and re-layouts: 2.7 us -> none  [the longest x2 2.57 us: weight_part(): return jnp.pad(flat, ((0, 0), (0, SLOT - share), (0, 0)))]
    dynamic_slice x1 -> x0, local copies, waits for them, and re-layouts: 1.32 us -> none  [past_part(): part = lax.dynamic_slice_in_dim(past, chip * 2 * share, 2 * share, axis=3)]
where the time goes in v2:
time: 81.4 us; the launch traced here: 81.3 us
  Pallas kernels  79.5 us (98%)
  local copies, waits for them, and re-layouts  1.72 us (2%)
    pallas_call x1, Pallas kernels, local(): pl.pallas_call(functools.partial(kernel, chips, bands, rows, cols, wide,...  79.5 us
    unnamed x1, local copies, waits for them, and re-layouts  1.72 us

profile of v2, /device:TPU:0, one launch (start us, length us, event | category | flops | bytes accessed | tf_op | source)
XLA Modules:
  0.0 81.3 jit_solution(12642510974133058408)
XLA Ops:
  0.0 79.5 %shard_map.136 = bf16[416,384]{1,0:T(8,128)(2,1)} custom-call(bf16[416,384]{1,0:T(8,128)(2,1)} %bitcast.7, bf16[2,4,104,384]{3,2,1,0:T(8,128)(2,1)} %past1.1, bf16[2,4,104,384]{3,2,1,0:T(8,128)(2,1)} %past2.1, bf16[27,48,384]{2,1,0:T(8,128)(2,1)} %bitcast.5, bf16[27,48,384]{2,1,0:T(8,128)(2,1)} %bitcast.6, f32[384]{0:T(512)} %bias1.1, f32[384]{0:T(512)} %bias2.1, ...), custom_call_target="tpu_custom_call" | custom-call | flops 7688159232 | bytes 8388608 | tf_op jit(solution)/shard_map/pallas_call | solution.py:502
  79.5 1.7 %copy.16 = bf16[1,4,104,384]{3,2,1,0:T(8,128)(2,1)} copy(bf16[1,4,104,384]{3,2,1,0:T(8,128)(2,1)} %bitcast.4) | data formatting | bytes 638976

commit v3 on v2

--- a/solution.py
+++ b/solution.py
@@ -12,6 +12,8 @@
 F32 = jnp.float32
 SLOT = 64
 LANES = 2 * SLOT
+GROUPS = ((1, 2), (0, 3))
+PIECES = ((1, 2), (0, 1), (3, 1))
 
 
 def normalize(v, gain):
@@ -37,9 +39,8 @@
     core = t % 2
     mate = t + 1 - 2 * core
     last = bands - 1
-    plane = chips == 4 and rows % 4 == 0
+    plane = chips == 4
     cells = rows * cols
-    half = rows // 2
     chans = video.shape[1]
     has_low = z > 0
     has_high = z < last
@@ -91,14 +92,16 @@
         select = jnp.where(chosen, 1.0, 0.0).astype(BF)
         return jnp.dot(flat, select, preferred_element_type=F32).astype(BF)
 
-    def put_stage(conv, h, values):
+    def put_stage(conv, g, values):
         spread = spread_of(values, 0, chips)
-        mine = pl.ds(h * half, half)
-        for q in range(chips):
-            stage[conv, q, mine] = spread[:, q * LANES : (q + 1) * LANES].reshape(
-                half, wide, LANES
-            )
-        act[conv, chip + 1, core, pl.ds(1 + h * half, half)] = stage[conv, chip, mine]
+        for i, r in enumerate(GROUPS[g]):
+            for q in range(chips):
+                stage[conv, q, r] = spread[i * wide : (i + 1) * wide, q * LANES : (q + 1) * LANES]
+            act[conv, chip + 1, core, r + 1] = stage[conv, chip, r]
+
+    def rows_of(cube, g):
+        first, second = GROUPS[g]
+        return jnp.concatenate([cube[first], cube[second]], axis=0)
 
     def fill_past():
         for conv, past in ((0, past1), (1, past2)):
@@ -118,29 +121,30 @@
 
     local_weight(0, w1).start()
     local_weight(1, w2).start()
-    vid = video[...].astype(F32)
-    active = silu(normalize(vid, gain1[...].reshape(1, chans)))
-    for h in range(2):
-        put_stage(0, h, active[h * half * cols : (h + 1) * half * cols])
+    vid = video[...].astype(F32).reshape(rows, cols, chans)
+    for g in range(2):
+        put_stage(0, g, silu(normalize(rows_of(vid, g), gain1[...].reshape(1, chans))))
 
     pl.semaphore_wait(
         barrier, chips + has_low.astype(jnp.int32) + has_high.astype(jnp.int32)
     )
 
-    def main_copy(conv, d, h):
+    def main_copy(conv, d, piece):
         q = peer(d)
-        return remote(
-            stage.at[conv, q, pl.ds(h * half, half)],
-            act.at[conv, chip + 1, core, pl.ds(1 + h * half, half)],
-            ms_sem.at[conv, d, h], mr_sem.at[conv, d, h], q * 2 + core, z,
-        )
-
-    def main_came(conv, d, h):
+        first, count = PIECES[piece]
+        return remote(
+            stage.at[conv, q, pl.ds(first, count)],
+            act.at[conv, chip + 1, core, pl.ds(first + 1, count)],
+            ms_sem.at[conv, d, piece], mr_sem.at[conv, d, piece], q * 2 + core, z,
+        )
+
+    def main_came(conv, d, piece):
         source = lax.rem(chip + chips - d, chips)
-        return remote(
-            stage.at[conv, 0, pl.ds(h * half, half)],
-            act.at[conv, source + 1, core, pl.ds(1 + h * half, half)],
-            ms_sem.at[conv, d, h], mr_sem.at[conv, d, h], mate, z,
+        first, count = PIECES[piece]
+        return remote(
+            stage.at[conv, 0, pl.ds(first, count)],
+            act.at[conv, source + 1, core, pl.ds(first + 1, count)],
+            ms_sem.at[conv, d, piece], mr_sem.at[conv, d, piece], mate, z,
         )
 
     def past_up(conv):
@@ -196,9 +200,9 @@
     def exchange(conv):
         if conv == 0:
             sent_weight(0, w1).start()
-            for h in range(2):
+            for piece in range(3):
                 for d in range(1, chips):
-                    main_copy(conv, d, h).start()
+                    main_copy(conv, d, piece).start()
             fill_past()
             for c in (0, 1):
 
@@ -210,22 +214,23 @@
                 def _():
                     past_down(c).start()
 
-        for d in range(1, chips):
-            main_came(conv, d, 0).wait_recv()
+        for piece in (1, 2, 0):
+            for d in range(1, chips):
+                main_came(conv, d, piece).wait_recv()
+
+        give_main(conv, core).start()
 
         @pl.when(has_low)
         def _():
             halo_down(conv).start()
 
-        for d in range(1, chips):
-            main_came(conv, d, 1).wait_recv()
-
         @pl.when(has_high)
         def _():
             halo_up(conv).start()
 
-        give_main(conv, core).start()
-
+        give_main(conv, 1 - core).wait_recv()
+
+    def pass_halo(conv):
         @pl.when(has_low)
         def _():
             halo_up(conv).wait_recv()
@@ -236,6 +241,7 @@
             halo_down(conv).wait_recv()
             give_halo(conv, 1, core).start()
 
+    def edges_came(conv):
         @pl.when(has_low)
         def _():
             past_up(conv).wait_recv()
@@ -246,108 +252,152 @@
             past_down(conv).wait_recv()
             give_halo(conv, 1, 1 - core).wait_recv()
 
-        give_main(conv, 1 - core).wait_recv()
-
-    def convolve(conv, consume):
-        def shift(n, _):
-            flat = act[conv, n // 2, n % 2].reshape((rows + 2) * wide, LANES).astype(F32)
-            size = (rows + 2) * wide
-            shifted[0, n] = pltpu.roll(flat, 1, 0).astype(BF).reshape(rows + 2, wide, LANES)
-            shifted[1, n] = pltpu.roll(flat, size - 1, 0).astype(BF).reshape(rows + 2, wide, LANES)
-            return 0
-
-        lax.fori_loop(0, 2 * (chips + 1), shift, 0)
-
-        def frame(q):
-            acc = jnp.zeros((rows * wide, chans), F32)
+    def convolve(conv, consume, between):
+        def shift_rows(first, count):
+            size = count * wide
+            mine = pl.ds(first, count)
+
+            def shift(n, _):
+                flat = act[conv, n // 2, n % 2, mine].reshape(size, LANES).astype(F32)
+                back = pltpu.roll(flat, 1, 0).astype(BF)
+                ahead = pltpu.roll(flat, size - 1, 0).astype(BF)
+                shifted[0, n, mine] = back.reshape(count, wide, LANES)
+                shifted[1, n, mine] = ahead.reshape(count, wide, LANES)
+                return 0
+
+            lax.fori_loop(0, 2 * (chips + 1), shift, 0)
+
+        def frame(q, g):
+            first, second = GROUPS[g]
+
+            def pair(load, r):
+                if second == first + 1:
+                    return load(first + r, 2).reshape(2 * wide, LANES)
+                return jnp.concatenate(
+                    [load(first + r, 1).reshape(wide, LANES), load(second + r, 1).reshape(wide, LANES)],
+                    axis=0,
+                )
+
+            acc = jnp.zeros((2 * wide, chans), F32)
             for tap in range(3):
                 n = 2 * q + core + tap
                 pieces = []
                 for r in range(3):
-                    pieces.append(shifted[0, n, r : r + rows].reshape(rows * wide, LANES))
-                    pieces.append(act[conv, n // 2, n % 2, r : r + rows].reshape(rows * wide, LANES))
-                    pieces.append(shifted[1, n, r : r + rows].reshape(rows * wide, LANES))
+                    pieces.append(pair(lambda a, c: shifted[0, n, a : a + c], r))
+                    pieces.append(pair(lambda a, c: act[conv, n // 2, n % 2, a : a + c], r))
+                    pieces.append(pair(lambda a, c: shifted[1, n, a : a + c], r))
                 acc = acc + jnp.dot(
                     jnp.concatenate(pieces, axis=1),
                     weights[conv, 9 * tap : 9 * tap + 9].reshape(9 * LANES, chans),
                     preferred_element_type=F32,
                 )
-            work[...] = acc.reshape(rows, wide, chans)[:, :cols]
+            acc = acc.reshape(2, wide, chans)[:, :cols]
+            work[first] = acc[0]
+            work[second] = acc[1]
 
         def sum_row(r):
             row_copy(conv, 0, r).wait_recv()
             psend[conv, 2, r] = (kept[r] + precv[conv, 0, r].astype(F32)).astype(BF)
             row_copy(conv, 2, r).start()
 
-        def plane_step(i, _):
-            x = (chip + 1 - i // 2) % 2
-            y = (chip // 2 + 1 - i % 2) % 2
-            frame(2 * y + x)
-
-            @pl.when(i == 0)
-            def _():
-                for r in range(rows):
-                    psend[conv, 0, r] = work[r].astype(BF)
-                    row_copy(conv, 0, r).start()
-
-            @pl.when(i == 1)
-            def _():
-                for r in range(0, rows, 2):
-                    psend[conv, 1, r] = work[r].astype(BF)
-                    if r < half:
-                        row_copy(conv, 1, r).start()
-                    kept[r + 1] = work[r + 1]
-
-            @pl.when(i == 2)
-            def _():
-                for r in range(0, rows, 2):
-                    psend[conv, 1, r + 1] = work[r + 1].astype(BF)
-                    if r + 1 < half:
-                        row_copy(conv, 1, r + 1).start()
-                    kept[r] = work[r]
-                for r in range(half):
-                    sum_row(r)
-                for r in range(half, rows):
-                    row_copy(conv, 1, r).start()
-
-            return 0
+        def plane_step(g, relay):
+            def run(i, _):
+                x = (chip + 1 - i // 2) % 2
+                y = (chip // 2 + 1 - i % 2) % 2
+                frame(2 * y + x, g)
+
+                @pl.when(i == 0)
+                def _():
+                    for r in GROUPS[g]:
+                        psend[conv, 0, r] = work[r].astype(BF)
+                        row_copy(conv, 0, r).start()
+
+                for i_of, parity in ((1, 0), (2, 1)):
+
+                    @pl.when(i == i_of)
+                    def _():
+                        for r in GROUPS[g]:
+                            if r % 2 == parity:
+                                psend[conv, 1, r] = work[r].astype(BF)
+                                row_copy(conv, 1, r).start()
+                            else:
+                                kept[r] = work[r]
+
+                if relay:
+
+                    @pl.when(i == 1)
+                    def _():
+                        pass_halo(conv)
+
+                @pl.when(i == 2)
+                def _():
+                    for r in GROUPS[g]:
+                        sum_row(r)
+
+                return 0
+
+            return run
+
+        def finish(g):
+            total_rows = []
+            for r in GROUPS[g]:
+                value = kept[r] if plane else work[r]
+                for kind in range(1 if plane else 0, chips - 1):
+                    if plane:
+                        row_copy(conv, kind, r).wait_recv()
+                    value = value + precv[conv, kind, r].astype(F32)
+                total_rows.append(value)
+            consume(g, jnp.concatenate(total_rows, axis=0))
 
         def step(d, _):
-            frame(peer(d))
+            for g in range(2):
+                frame(peer(d), g)
             psend[conv, d - 1] = work[...].astype(BF)
             part_copy(conv, d).start()
             return 0
 
+        shift_rows(1, rows)
         if plane:
-            lax.fori_loop(0, 4, plane_step, 0)
-            for r in range(half, rows):
-                sum_row(r)
+            lax.fori_loop(0, 4, plane_step(0, True), 0)
+            for r in GROUPS[0]:
+                kept[r] = work[r]
+            edges_came(conv)
+            shift_rows(0, 1)
+            shift_rows(rows + 1, 1)
+            lax.fori_loop(0, 3, plane_step(1, False), 0)
+            finish(0)
+            frame(chip, 1)
+            for r in GROUPS[1]:
+                kept[r] = work[r]
+            between()
+            finish(1)
         else:
+            pass_halo(conv)
+            edges_came(conv)
+            shift_rows(0, 1)
+            shift_rows(rows + 1, 1)
             lax.fori_loop(1, chips, step, 0)
-            frame(chip)
+            for g in range(2):
+                frame(chip, g)
             for d in range(1, chips):
                 part_copy(conv, d).wait_recv()
-        for h in range(2):
-            mine = slice(h * half, (h + 1) * half)
-            for kind in range(1 if plane else 0, chips - 1):
-                if plane:
-                    for r in range(h * half, (h + 1) * half):
-                        row_copy(conv, kind, r).wait_recv()
-                work[mine] += precv[conv, kind, mine].astype(F32)
-            consume(h, work[mine].reshape(half * cols, chans))
+            finish(0)
+            between()
+            finish(1)
 
     exchange(0)
     sent_weight(1, w2).start()
     local_weight(0, w1).wait()
     remote(w1, weight_slot(0, 1 - core), ws_sem.at[0], wr_sem.at[0], mate, z).wait_recv()
 
-    def after_first(h, summed):
+    def after_first(g, summed):
         hidden = summed + bias1[...].reshape(1, chans)
-        put_stage(1, h, silu(normalize(hidden, gain2[...].reshape(1, chans))))
-        for d in range(1, chips):
-            main_copy(1, d, h).start()
-
-    convolve(0, after_first)
+        put_stage(1, g, silu(normalize(hidden, gain2[...].reshape(1, chans))))
+        for piece in (0,) if g == 0 else (1, 2):
+            for d in range(1, chips):
+                main_copy(1, d, piece).start()
+
+    convolve(0, after_first, lambda: None)
     exchange(1)
     local_weight(1, w2).wait()
     remote(w2, weight_slot(1, 1 - core), ws_sem.at[1], wr_sem.at[1], mate, z).wait_recv()
@@ -362,22 +412,41 @@
             held.at[b, h], held.at[b, h], xleft_sem.at[b, h], xr_sem.at[b, h], t, z - 1
         )
 
-    def after_second(h, summed):
-        mine = slice(h * half * cols, (h + 1) * half * cols)
+    def after_second(g, summed):
         conv_out = summed + bias2[...].reshape(1, chans)
-        block = (video[mine].astype(F32) + conv_out).astype(BF)
-        out[mine] = block
-        held[z, h] = normalize(block.astype(F32), gain3[...].reshape(1, chans)).astype(BF)
+        before = rows_of(video[...].astype(F32).reshape(rows, cols, chans), g)
+        block = (before + conv_out).astype(BF)
+        wider = block.astype(F32)
+        for i, r in enumerate(GROUPS[g]):
+            out[r] = wider[i * cols : (i + 1) * cols].astype(BF)
+        held[z, g] = normalize(wider, gain3[...].reshape(1, chans)).astype(BF)
 
         @pl.when(has_high)
         def _():
-            right(z, h).start()
+            right(z, g).start()
 
         @pl.when(has_low)
         def _():
-            left(z, h).start()
-
-    convolve(1, after_second)
+            left(z, g).start()
+
+    def relay(k, g):
+        @pl.when(z - k >= 0)
+        def _():
+            right(z - k, g).wait_recv()
+
+            @pl.when(has_high)
+            def _():
+                right(z - k, g).start()
+
+        @pl.when(z + k < bands)
+        def _():
+            left(z + k, g).wait_recv()
+
+            @pl.when(has_low)
+            def _():
+                left(z + k, g).start()
+
+    convolve(1, after_second, lambda: relay(1, 0))
     factor = 1.0 / (float(chans) ** 0.5)
     queries[...] = jnp.dot(held[z].reshape(cells, chans), wq[...], preferred_element_type=F32).astype(BF)
     top[...] = jnp.full(top.shape, -jnp.inf, F32)
@@ -404,23 +473,11 @@
     attend(z)
 
     def ring(k, _):
-        for h in range(2):
-
-            @pl.when(z - k >= 0)
-            def _():
-                right(z - k, h).wait_recv()
-
-                @pl.when(has_high)
-                def _():
-                    right(z - k, h).start()
-
-            @pl.when(z + k < bands)
-            def _():
-                left(z + k, h).wait_recv()
-
-                @pl.when(has_low)
-                def _():
-                    left(z + k, h).start()
+        @pl.when(k > 1)
+        def _():
+            relay(k, 0)
+
+        relay(k, 1)
 
         @pl.when(z - k >= 0)
         def _():
@@ -434,9 +491,11 @@
 
     lax.fori_loop(1, bands, ring, 0)
     att = (accum[...] / total[...]).astype(BF)
-    out[...] = (
-        out[...].astype(F32) + jnp.dot(att, wo[...], preferred_element_type=F32)
-    ).astype(BF)
+    projected = jnp.dot(att, wo[...], preferred_element_type=F32)
+    for g in range(2):
+        for i, r in enumerate(GROUPS[g]):
+            first = (2 * g + i) * cols
+            out[r] = (out[r].astype(F32) + projected[first : first + cols]).astype(BF)
 
     def drain(b, _):
         @pl.when(jnp.logical_and(has_high, b <= z))
@@ -456,8 +515,8 @@
         sent_weight(conv, w).wait_send()
         give_main(conv, core).wait_send()
         for d in range(1, chips):
-            for h in range(2):
-                main_copy(conv, d, h).wait_send()
+            for piece in range(3):
+                main_copy(conv, d, piece).wait_send()
             if plane:
                 for r in range(rows):
                     row_copy(conv, d - 1, r).wait_send()
@@ -501,7 +560,7 @@
     flops = 2 * 2 * cells * 27 * chans * chans + 4 * cells * cells * bands * chans
     encoded = pl.pallas_call(
         functools.partial(kernel, chips, bands, rows, cols, wide, share, direct),
-        out_shape=jax.ShapeDtypeStruct((cells, chans), BF),
+        out_shape=jax.ShapeDtypeStruct((rows, cols, chans), BF),
         in_specs=[vmem] * 3 + [hbm] * 2 + [vmem] * 9,
         out_specs=vmem,
         scratch_shapes=[
@@ -519,7 +578,7 @@
             pltpu.VMEM((cells, 1), F32),
             pltpu.VMEM((cells, chans), F32),
             dma((2,)), dma((2,)), dma((2,)),
-            dma((2, chips, 2)), dma((2, chips, 2)),
+            dma((2, chips, 3)), dma((2, chips, 3)),
             dma((2, 2)), dma((2, 2)), dma((2, 2)), dma((2, 2)),
             dma((2,)), dma((2,)), dma((2, 2)), dma((2, 2)),
             dma((2, chips, rows)), dma((2, chips, rows)),

time: 81.4 us -> 78.4 us (0.963)
  Pallas kernels: 79.5 us -> 76.4 us
    pallas_call x1, Pallas kernels: 79.5 us -> 76.4 us  [local(): pl.pallas_call(functools.partial(kernel, chips, bands, rows, cols, wide,...]
where the time goes in v3:
time: 78.4 us; the launch traced here: 78.2 us
  Pallas kernels  76.4 us (97%)
  local copies, waits for them, and re-layouts  1.72 us (2%)
    pallas_call x1, Pallas kernels, local(): pl.pallas_call(functools.partial(kernel, chips, bands, rows, cols, wide,...  76.4 us
    unnamed x1, local copies, waits for them, and re-layouts  1.72 us

profile of v3, /device:TPU:0, one launch (start us, length us, event | category | flops | bytes accessed | tf_op | source)
XLA Modules:
  0.0 78.2 jit_solution(9039041363664302834)
XLA Ops:
  0.0 76.4 %shard_map.136 = bf16[4,104,384]{2,1,0:T(8,128)(2,1)} custom-call(bf16[416,384]{1,0:T(8,128)(2,1)} %bitcast.7, bf16[2,4,104,384]{3,2,1,0:T(8,128)(2,1)} %past1.1, bf16[2,4,104,384]{3,2,1,0:T(8,128)(2,1)} %past2.1, bf16[27,48,384]{2,1,0:T(8,128)(2,1)} %bitcast.5, bf16[27,48,384]{2,1,0:T(8,128)(2,1)} %bitcast.6, f32[384]{0:T(512)} %bias1.1, f32[384]{0:T(512)} %bias2.1, ...), custom_call_target="tpu_custom_call" | custom-call | flops 7688159232 | bytes 8388608 | tf_op jit(solution)/shard_map/pallas_call | solution.py:561
  76.5 1.7 %copy.16 = bf16[1,4,104,384]{3,2,1,0:T(8,128)(2,1)} copy(bf16[1,4,104,384]{3,2,1,0:T(8,128)(2,1)} %bitcast.4) | data formatting | bytes 638976

commit v4 on v3

--- a/solution.py
+++ b/solution.py
@@ -29,7 +29,7 @@
     share, direct,
     video, past1, past2, w1, w2, bias1, bias2, gain1, gain2, gain3,
     wq, wk, wv, wo, out,
-    weights, stage, act, shifted, psend, precv, work, kept, held, queries, top, total, accum,
+    select, weights, stage, act, shifted, psend, precv, work, kept, held, queries, top, total, accum,
     wl_sem, ws_sem, wr_sem, ms_sem, mr_sem, hs_sem, hr_sem, qs_sem, qr_sem,
     fs_sem, fr_sem, gs_sem, gr_sem, ps_sem, pr_sem, xr_sem, xright_sem, xleft_sem,
 ):
@@ -79,18 +79,25 @@
             w, weight_slot(conv, core), ws_sem.at[conv], wr_sem.at[conv], mate, z
         )
 
+    lane = lax.broadcasted_iota(jnp.int32, (chans, LANES), 1)
+    upper = lane >= SLOT
+    within = jnp.where(upper, lane - SLOT, lane)
+    offset = lax.broadcasted_iota(jnp.int32, (chans, LANES), 0) - within
+    offset = jnp.where(upper, offset - share, offset)
+    offset = jnp.where(within < share, offset, -1)
+    for q in range(chips + 1):
+        owner = q if q < chips else chip
+        select[:, q * LANES : (q + 1) * LANES] = jnp.where(
+            offset == 2 * share * owner, 1.0, 0.0
+        ).astype(BF)
+
     def spread_of(values, first, count):
         lead = values.shape[0] // cols
         cube = values.reshape(lead, cols, chans)
         cube = jnp.concatenate([cube, jnp.zeros((lead, wide - cols, chans), F32)], axis=1)
         flat = cube.reshape(lead * wide, chans).astype(BF)
-        channel = lax.broadcasted_iota(jnp.int32, (chans, count * LANES), 0)
-        lane = lax.broadcasted_iota(jnp.int32, (chans, count * LANES), 1)
-        within = lane % SLOT
-        source = (lane // SLOT + 2 * first) * share + within
-        chosen = jnp.logical_and(channel == source, within < share)
-        select = jnp.where(chosen, 1.0, 0.0).astype(BF)
-        return jnp.dot(flat, select, preferred_element_type=F32).astype(BF)
+        chosen = select[:, first * LANES : (first + count) * LANES]
+        return jnp.dot(flat, chosen, preferred_element_type=F32).astype(BF)
 
     def put_stage(conv, g, values):
         spread = spread_of(values, 0, chips)
@@ -106,7 +113,7 @@
     def fill_past():
         for conv, past in ((0, past1), (1, past2)):
             for n in range(2):
-                part = spread_of(past[n].reshape(cells, chans).astype(F32), chip, 1)
+                part = spread_of(past[n].reshape(cells, chans).astype(F32), chips, 1)
                 act[conv, 0, n, 1 : rows + 1] = part.reshape(rows, wide, LANES)
             if direct:
                 weights[conv, :, :, share:] = jnp.zeros((27, 2, SLOT - share, chans), BF)
@@ -172,9 +179,10 @@
             hs_sem.at[conv, 1], hr_sem.at[conv, 1], t, z - 1,
         )
 
-    def give_main(conv, whose):
-        part = act.at[conv, pl.ds(1, chips), whose, pl.ds(1, rows)]
-        return remote(part, part, fs_sem.at[conv], fr_sem.at[conv], mate, z)
+    def give_main(conv, piece, whose):
+        first, count = PIECES[piece]
+        part = act.at[conv, pl.ds(1, chips), whose, pl.ds(first + 1, count)]
+        return remote(part, part, fs_sem.at[conv, piece], fr_sem.at[conv, piece], mate, z)
 
     def give_halo(conv, side, whose):
         part = act.at[conv, pl.ds(1, chips), whose, side * (rows + 1)]
@@ -214,11 +222,10 @@
                 def _():
                     past_down(c).start()
 
-        for piece in (1, 2, 0):
+        for piece in range(3):
             for d in range(1, chips):
                 main_came(conv, d, piece).wait_recv()
-
-        give_main(conv, core).start()
+            give_main(conv, piece, core).start()
 
         @pl.when(has_low)
         def _():
@@ -228,7 +235,8 @@
         def _():
             halo_up(conv).start()
 
-        give_main(conv, 1 - core).wait_recv()
+        for piece in range(3):
+            give_main(conv, piece, 1 - core).wait_recv()
 
     def pass_halo(conv):
         @pl.when(has_low)
@@ -513,7 +521,8 @@
     lax.fori_loop(0, bands, drain, 0)
     for conv, w in ((0, w1), (1, w2)):
         sent_weight(conv, w).wait_send()
-        give_main(conv, core).wait_send()
+        for piece in range(3):
+            give_main(conv, piece, core).wait_send()
         for d in range(1, chips):
             for piece in range(3):
                 main_copy(conv, d, piece).wait_send()
@@ -564,6 +573,7 @@
         in_specs=[vmem] * 3 + [hbm] * 2 + [vmem] * 9,
         out_specs=vmem,
         scratch_shapes=[
+            pltpu.VMEM((chans, (chips + 1) * LANES), BF),
             pltpu.VMEM((2, 27, 2, SLOT, chans), BF),
             pltpu.VMEM((2, chips, rows, wide, LANES), BF),
             pltpu.VMEM((2, chips + 1, 2, rows + 2, wide, LANES), BF),
@@ -580,7 +590,7 @@
             dma((2,)), dma((2,)), dma((2,)),
             dma((2, chips, 3)), dma((2, chips, 3)),
             dma((2, 2)), dma((2, 2)), dma((2, 2)), dma((2, 2)),
-            dma((2,)), dma((2,)), dma((2, 2)), dma((2, 2)),
+            dma((2, 3)), dma((2, 3)), dma((2, 2)), dma((2, 2)),
             dma((2, chips, rows)), dma((2, chips, rows)),
             dma((bands, 2)), dma((bands, 2)), dma((bands, 2)),
         ],

time: 78.4 us -> 78.8 us (level)
  no operation moved by 1% of the time
where the time goes in v4:
time: 78.8 us; the launch traced here: 78.6 us
  Pallas kernels  76.9 us (98%)
  local copies, waits for them, and re-layouts  1.72 us (2%)
    pallas_call x1, Pallas kernels, local(): pl.pallas_call(functools.partial(kernel, chips, bands, rows, cols, wide,...  76.9 us
    unnamed x1, local copies, waits for them, and re-layouts  1.72 us

profile of v4, /device:TPU:0, one launch (start us, length us, event | category | flops | bytes accessed | tf_op | source)
XLA Modules:
  0.0 78.6 jit_solution(5045928336300789560)
XLA Ops:
  0.0 76.9 %shard_map.136 = bf16[4,104,384]{2,1,0:T(8,128)(2,1)} custom-call(bf16[416,384]{1,0:T(8,128)(2,1)} %bitcast.7, bf16[2,4,104,384]{3,2,1,0:T(8,128)(2,1)} %past1.1, bf16[2,4,104,384]{3,2,1,0:T(8,128)(2,1)} %past2.1, bf16[27,48,384]{2,1,0:T(8,128)(2,1)} %bitcast.5, bf16[27,48,384]{2,1,0:T(8,128)(2,1)} %bitcast.6, f32[384]{0:T(512)} %bias1.1, f32[384]{0:T(512)} %bias2.1, ...), custom_call_target="tpu_custom_call" | custom-call | flops 7688159232 | bytes 8388608 | tf_op jit(solution)/shard_map/pallas_call | solution.py:570
  76.9 1.7 %copy.16 = bf16[1,4,104,384]{3,2,1,0:T(8,128)(2,1)} copy(bf16[1,4,104,384]{3,2,1,0:T(8,128)(2,1)} %bitcast.4) | data formatting | bytes 638976

commit v5 on v3

--- a/solution.py
+++ b/solution.py
@@ -364,8 +364,9 @@
             edges_came(conv)
             shift_rows(0, 1)
             shift_rows(rows + 1, 1)
-            lax.fori_loop(0, 3, plane_step(1, False), 0)
+            lax.fori_loop(0, 2, plane_step(1, False), 0)
             finish(0)
+            lax.fori_loop(2, 3, plane_step(1, False), 0)
             frame(chip, 1)
             for r in GROUPS[1]:
                 kept[r] = work[r]

time: 78.4 us -> 79.7 us (1.017)
  Pallas kernels: 76.4 us -> 77.8 us
    pallas_call x1, Pallas kernels: 76.4 us -> 77.8 us  [local(): pl.pallas_call(functools.partial(kernel, chips, bands, rows, cols, wide,...]
where the time goes in v5:
time: 79.7 us; the launch traced here: 79.5 us
  Pallas kernels  77.8 us (98%)
  local copies, waits for them, and re-layouts  1.72 us (2%)
    pallas_call x1, Pallas kernels, local(): pl.pallas_call(functools.partial(kernel, chips, bands, rows, cols, wide,...  77.8 us
    unnamed x1, local copies, waits for them, and re-layouts  1.72 us

profile of v5, /device:TPU:0, one launch (start us, length us, event | category | flops | bytes accessed | tf_op | source)
XLA Modules:
  0.0 79.5 jit_solution(4863823414622993729)
XLA Ops:
  0.0 77.8 %shard_map.136 = bf16[4,104,384]{2,1,0:T(8,128)(2,1)} custom-call(bf16[416,384]{1,0:T(8,128)(2,1)} %bitcast.7, bf16[2,4,104,384]{3,2,1,0:T(8,128)(2,1)} %past1.1, bf16[2,4,104,384]{3,2,1,0:T(8,128)(2,1)} %past2.1, bf16[27,48,384]{2,1,0:T(8,128)(2,1)} %bitcast.5, bf16[27,48,384]{2,1,0:T(8,128)(2,1)} %bitcast.6, f32[384]{0:T(512)} %bias1.1, f32[384]{0:T(512)} %bias2.1, ...), custom_call_target="tpu_custom_call" | custom-call | flops 7688159232 | bytes 8388608 | tf_op jit(solution)/shard_map/pallas_call | solution.py:562
  77.8 1.7 %copy.16 = bf16[1,4,104,384]{3,2,1,0:T(8,128)(2,1)} copy(bf16[1,4,104,384]{3,2,1,0:T(8,128)(2,1)} %bitcast.4) | data formatting | bytes 638976
